TPU v7x, 32 devices: a whole 2x2x4 slice. The times are simulated.
32 devices in a mesh: dp: 4 (over x, core), ctx: 8 (over z, y).
Axes of the slice: x: 2, y: 2, z: 4, core: 2. Of those that a mesh axis runs over, the one named last changes fastest.
Arguments:
- hidden_in: bfloat16 [4, 1024, 2048], P('dp', 'ctx')
- grad_out: bfloat16 [4, 1024, 2048], P('dp', 'ctx'), may hold values from -6 to 6
- seg_len: int32 [4, 9], P('dp'), may hold values from 32 to 512, as said below
- seg_parent: int32 [4, 9], P('dp'), may hold values from 0 to 7, as said below
- gain_attn: bfloat16 [2048], replicated, may hold values from 0.5 to 1.5
- shift_attn: bfloat16 [2048], replicated, may hold values from -1 to 1
- w_qkv: bfloat16 [6144, 2048], P('ctx'), may hold values from -0.125 to 0.125
- bias_qkv: bfloat16 [6144], replicated, may hold values from -1 to 1
- w_out: bfloat16 [2048, 2048], P('ctx'), may hold values from -1 to 1
- bias_out: bfloat16 [2048], replicated, may hold values from -1 to 1
- gain_mlp: bfloat16 [2048], replicated, may hold values from 0.5 to 1.5
- shift_mlp: bfloat16 [2048], replicated, may hold values from -1 to 1
- w_up: bfloat16 [8192, 2048], P('ctx'), may hold values from -0.125 to 0.125
- bias_up: bfloat16 [8192], replicated, may hold values from -1 to 1
- w_down: bfloat16 [8192, 2048], P('ctx'), may hold values from -0.0625 to 0.0625
- bias_down: bfloat16 [2048], replicated, may hold values from -1 to 1
Outputs:
- hidden_out: bfloat16 [4, 1024, 2048], P('dp', 'ctx')
- grad_in: float32 [4, 1024, 2048], P('dp', 'ctx')
- grad_gain_attn: float32 [2048], replicated
- grad_shift_attn: float32 [2048], replicated
- grad_w_qkv: float32 [6144, 2048], P('ctx')
- grad_bias_qkv: float32 [6144], replicated
- grad_w_out: float32 [2048, 2048], P('ctx')
- grad_bias_out: float32 [2048], replicated
- grad_gain_mlp: float32 [2048], replicated
- grad_shift_mlp: float32 [2048], replicated
- grad_w_up: float32 [8192, 2048], P('ctx')
- grad_bias_up: float32 [8192], replicated
- grad_w_down: float32 [8192, 2048], P('ctx')
- grad_bias_down: float32 [2048], replicated
Inputs may be any that keep to these rules, and one draw needn't show every extreme that they name: `seg_len`: lengths of a tree's 9 segments in stored order; they sum to 1024; segment 0, the trunk, holds 256 to 512 tokens, and in every draw some tree's trunk holds exactly 512; every other segment holds 32 or more. `seg_parent`: segment 0 is its own parent; four segments are branches with parent 0; each of the four others is a leaf whose parent is a branch stored before it, one leaf to a branch.
All inputs are finite; a program needn't handle non-finite values.
Results may differ from a plain program's by a relative error of at most 0.015.
Values may be sent and summed in bfloat16 or wider, within the bound.
A program may use at most 960 MiB of HBM per device.

v0:
```python
import functools
import math

import jax
import jax.numpy as jnp
from jax import lax
from jax.experimental import pallas as pl
from jax.experimental.pallas import tpu as pltpu
from jax.sharding import PartitionSpec as P

D = 2048
HEADS = 16
HEAD_DIM = 128
ROT_DIM = 32
FF = 8192

norm_eps = 1e-05
masked_score = -1e30
f32 = jnp.float32
bf16 = jnp.bfloat16


def dot_nt(a, b):
    return lax.dot_general(a, b, (((1,), (1,)), ((), ())), preferred_element_type=f32)


def dot_nn(a, b):
    return lax.dot_general(a, b, (((1,), (0,)), ((), ())), preferred_element_type=f32)


def dot_tn(a, b):
    return lax.dot_general(a, b, (((0,), (0,)), ((), ())), preferred_element_type=f32)


MESH = pl.DeviceIdType.MESH
RAILS = 2


def place(group):
    dp = lax.axis_index("dp")
    ctx = lax.axis_index("ctx")
    return dp, ctx, ctx // RAILS, ctx % RAILS, group // RAILS


def copy_to(src, dst, send, recv, device):
    return pltpu.make_async_remote_copy(
        src_ref=src,
        dst_ref=dst,
        send_sem=send,
        recv_sem=recv,
        device_id=device,
        device_id_type=MESH,
    )


def signal(device):
    barrier = pltpu.get_barrier_semaphore()
    pl.semaphore_signal(barrier, inc=1, device_id=device, device_id_type=MESH)


def arrive(count):
    pl.semaphore_wait(pltpu.get_barrier_semaphore(), count)


def pair_order(z, depth):
    return [
        z,
        jnp.where(z > 0, z - 1, 1),
        jnp.where(z == depth - 1, 1, jnp.where(z == depth - 2, depth - 1, 2)),
        jnp.where(z < depth // 2, depth - 1, 0),
    ]


def layer_kernel(group, *refs):
    hidden, grad, w_up_in, w_down_in, w_qkv_in, w_out = refs[:6]
    norms, bias_up, bias_qkv, inverse, seg_len, seg_parent = refs[6:12]
    h_out, g_out, x_out, heads_out, part_out, back_out, pairs_out, cols_out = refs[12:20]
    tables, sums, bias_sum = refs[20:23]
    h_buf, g_buf, w_up, w_down, w_qkv, x_mlp, x_attn, act, slope, pre_grad = refs[23:33]
    heads, part, back, down_grad, up_grad, core_buf, mean, rstd = refs[33:41]
    own_sem, y_send, y_recv, up_send, up_recv, down_send, down_recv = refs[41:48]
    weight_sem, pair_sem, grad_sem, head_send, head_recv = refs[48:53]
    core_send, core_recv, cols_send, cols_recv = refs[53:57]
    dp, ctx, z, y, depth = place(group)
    bufs, sources, outs = (h_buf, g_buf), (hidden, grad), (h_out, g_out)
    rows = hidden.shape[0]
    pair_rows = RAILS * rows
    tokens, columns = h_buf.shape
    units = act.shape[1]
    head_cols = heads.shape[2]
    other = (dp, z * RAILS + 1 - y)
    above = (dp, jnp.minimum(z + 1, depth - 1) * RAILS + y)
    below = (dp, jnp.maximum(z - 1, 0) * RAILS + y)
    has_above, has_below = z < depth - 1, z > 0
    order = pair_order(z, depth)

    x, core = dp // 2, dp % 2
    sibling = (x * 2 + 1 - core, ctx)
    across = ((1 - x) * 2 + core, ctx)

    for n in range(1, group):
        signal((dp, lax.rem(ctx + n, group)))
    signal(sibling)
    signal(across)
    arrive(group + 1)

    def chunk(i, at_z, at_y):
        start = pl.multiple_of((at_z * RAILS + at_y) * rows, rows)
        return bufs[i].at[pl.ds(start, rows)]

    def to_other(i, at_z, source=None):
        here = chunk(i, at_z, y)
        return copy_to(
            here if source is None else source, here, y_send.at[i, at_z], y_recv.at[i, at_z], other
        )

    def upward(i, at_z, source=None):
        here = chunk(i, at_z, y)
        return copy_to(
            here if source is None else source,
            here,
            up_send.at[i, at_z],
            up_recv.at[i, at_z],
            above,
        )

    def downward(i, at_z, source=None):
        here = chunk(i, at_z, y)
        return copy_to(
            here if source is None else source,
            here,
            down_send.at[i, at_z],
            down_recv.at[i, at_z],
            below,
        )

    def relay(i, k):
        @pl.when(z >= k)
        def _():
            at_z = jnp.maximum(z - k, 0)
            upward(i, at_z).wait_recv()
            pl.when(has_above)(lambda: upward(i, at_z).start())

        @pl.when(z + k < depth)
        def _():
            at_z = jnp.minimum(z + k, depth - 1)
            downward(i, at_z).wait_recv()
            pl.when(has_below)(lambda: downward(i, at_z).start())

    def turn(n):
        if n < depth:
            relay(0, n)
            pl.when((z == n - 1) & has_above)(lambda: upward(1, z, sources[1]).start())
            pl.when((z == depth - n) & has_below)(lambda: downward(1, z, sources[1]).start())
            to_other(0, order[n]).start()
        else:
            if n < 2 * depth - 1:
                relay(1, n - depth + 1)
            if n == depth:
                to_other(1, z, sources[1]).start()
            else:
                to_other(1, order[n - depth]).start()

    def y_arrive(i, s):
        here = chunk(i, order[s], 1 - y)
        copy_to(
            here, here, y_send.at[i, order[s]], y_recv.at[i, order[s]], other
        ).wait_recv()

    def pair_at(s):
        return pl.ds(pl.multiple_of(order[s] * pair_rows, pair_rows), pair_rows)

    def keep(n, s, buf, out):
        at = pair_at(s)
        return pltpu.make_async_copy(buf.at[at], out.at[at], pair_sem.at[n, s])

    own = [pltpu.make_async_copy(sources[i], chunk(i, z, y), own_sem.at[i]) for i in range(2)]
    weights = [
        pltpu.make_async_copy(source, held, weight_sem.at[n])
        for n, (source, held) in enumerate(
            ((w_up_in, w_up), (w_qkv_in, w_qkv), (w_down_in, w_down))
        )
    ]
    own[0].start()
    to_other(0, z, sources[0]).start()
    pl.when(has_above)(lambda: upward(0, z, sources[0]).start())
    pl.when(has_below)(lambda: downward(0, z, sources[0]).start())
    for copy in weights:
        copy.start()
    own[1].start()

    starts, shifts = [], []
    at = jnp.int32(0)
    for n in range(seg_len.shape[1]):
        parent = seg_parent[0, n]
        grand = seg_parent[0, parent]
        before = jnp.where(parent != n, seg_len[0, parent], 0) + jnp.where(
            (grand != n) & (grand != parent), seg_len[0, grand], 0
        )
        starts.append(at)
        shifts.append(before - at)
        at = at + seg_len[0, n]

    turned_half = ROT_DIM // 2

    @pl.loop(0, tokens // rows)
    def _(n):
        at = pl.ds(pl.multiple_of(n * rows, rows), rows)
        token = n * rows + lax.broadcasted_iota(jnp.int32, (turned_half, rows), 1)
        position = token + shifts[0]
        for m in range(1, len(starts)):
            position = position + jnp.where(token >= starts[m], shifts[m] - shifts[m - 1], 0)
        angle = position.astype(f32) * inverse[...]
        cosine, sine = jnp.cos(angle), jnp.sin(angle)
        still = jnp.zeros((HEAD_DIM - ROT_DIM, rows), f32)
        none = jnp.zeros((turned_half, rows), f32)
        tables[0, at, :] = jnp.concatenate([cosine, cosine, still + 1.0], axis=0).T
        tables[1, at, :] = jnp.concatenate([-sine, none, still], axis=0).T
        tables[2, at, :] = jnp.concatenate([none, sine, still], axis=0).T

    sums[...] = jnp.zeros_like(sums)
    bias_sum[...] = jnp.zeros_like(bias_sum)

    def normalize(s):
        step = 32

        @pl.loop(0, pair_rows // step)
        def _(n):
            at = pl.ds(pl.multiple_of(order[s] * pair_rows + n * step, step), step)
            values = h_buf[at, :].astype(f32)
            average = jnp.mean(values, axis=1, keepdims=True)
            centred = values - average
            spread = lax.rsqrt(jnp.mean(centred * centred, axis=1, keepdims=True) + norm_eps)
            normed = centred * spread
            x_attn[at, :] = (normed * norms[0:1, :] + norms[1:2, :]).astype(bf16)
            x_mlp[at, :] = (normed * norms[2:3, :] + norms[3:4, :]).astype(bf16)
            mean[at, :] = average
            rstd[at, :] = spread
            lane = lax.broadcasted_iota(jnp.int32, (step, HEAD_DIM), 1)
            tables[3, at, :] = jnp.where(lane == 0, average, spread)

    wide = 512

    def feed(s):
        at = pair_at(s)

        @pl.loop(0, units // wide)
        def _(n):
            cols = pl.ds(pl.multiple_of(n * wide, wide), wide)
            pre = dot_nt(x_mlp[at, :], w_up[cols, :]) + bias_up[:, cols]
            normal_cdf = 0.5 * (1.0 + lax.erf(pre * math.sqrt(0.5)))
            act[at, cols] = (pre * normal_cdf).astype(bf16)
            slope[at, cols] = (
                normal_cdf + pre * jnp.exp(-0.5 * pre * pre) * (1.0 / math.sqrt(2.0 * math.pi))
            ).astype(slope.dtype)

    def project(s):
        at = pair_at(s)
        for j in range(3):
            block = pl.ds(j * head_cols, head_cols)
            raw = dot_nt(x_attn[at, :], w_qkv[block, :]) + bias_qkv[:, block]
            turns = lax.div(3 * ctx + j, group) < 2
            for m in range(head_cols // HEAD_DIM):
                one = raw[:, m * HEAD_DIM : (m + 1) * HEAD_DIM]
                turned = (
                    one * tables[0, at, :]
                    + pltpu.roll(one, HEAD_DIM - ROT_DIM // 2, 1) * tables[1, at, :]
                    + pltpu.roll(one, ROT_DIM // 2, 1) * tables[2, at, :]
                )
                heads[j, at, m * HEAD_DIM : (m + 1) * HEAD_DIM] = jnp.where(
                    turns, turned, one
                ).astype(bf16)

    def mix(s):
        at = pair_at(s)

        @pl.loop(0, columns // wide)
        def _(n):
            cols = pl.ds(pl.multiple_of(n * wide, wide), wide)
            part[at, cols] = dot_nn(act[at, :], w_down[:, cols]).astype(bf16)

    def back_feed(s):
        at = pair_at(s)

        @pl.loop(0, units // wide)
        def _(n):
            cols = pl.ds(pl.multiple_of(n * wide, wide), wide)
            rounded = (
                dot_nt(g_buf[at, :], w_down[cols, :]) * slope[at, cols].astype(f32)
            ).astype(bf16)
            pre_grad[at, cols] = rounded
            bias_sum[:, cols] += jnp.sum(rounded.astype(f32), axis=0, keepdims=True)

        @pl.loop(0, columns // wide)
        def _(n):
            cols = pl.ds(pl.multiple_of(n * wide, wide), wide)
            entry = dot_nn(pre_grad[at, :], w_up[:, cols])
            normed = (h_buf[at, cols].astype(f32) - mean[at, :]) * rstd[at, :]
            sums[0:1, cols] += jnp.sum(entry * normed, axis=0, keepdims=True)
            sums[1:2, cols] += jnp.sum(entry, axis=0, keepdims=True)
            back[at, cols] = (entry * norms[2:3, cols]).astype(bf16)

    def forward(s):
        keep(0, s, h_buf, h_out).start()
        normalize(s)
        keep(1, s, x_attn, x_out).start()
        if s == 0:
            weights[0].wait()
        feed(s)
        if s == 0:
            weights[1].wait()
        project(s)

    def backward(s):
        keep(2, s, g_buf, g_out).start()
        if s == 0:
            weights[2].wait()
        mix(s)
        keep(3, s, part, part_out).start()
        back_feed(s)
        keep(4, s, back, back_out).start()

    tall = 256
    half = core_buf.shape[1]
    tiles = units // tall
    held = (down_grad, up_grad)

    def grad_half(t, which):
        start = pl.multiple_of((t % tiles) * tall + which * half, half)
        return held[t // tiles].at[pl.ds(start, half)]

    def to_core(t):
        return copy_to(
            grad_half(t, 1 - core), core_buf.at[t], core_send.at[t], core_recv.at[t], sibling
        )

    def grad_keep(t):
        return pltpu.make_async_copy(
            grad_half(t, core), pairs_out.at[pl.ds(t * half, half)], grad_sem.at[t]
        )

    def outer(n, left, right):
        for m in range(tiles):
            mine = pl.ds(m * tall, tall)

            @pl.loop(0, columns // (2 * wide))
            def _(k):
                cols = pl.ds(pl.multiple_of(k * 2 * wide, 2 * wide), 2 * wide)
                held[n][mine, cols] = dot_tn(left[:, mine], right[:, cols]).astype(bf16)

            to_core(n * tiles + m).start()

    def outer_sum(n):
        for t in range(n * tiles, (n + 1) * tiles):
            to_core(t).wait_recv()
            mine = grad_half(t, core)

            @pl.loop(0, half // 32)
            def _(k):
                at = pl.ds(pl.multiple_of(k * 32, 32), 32)
                mine[at, :] = (mine[at, :].astype(f32) + core_buf[t, at, :].astype(f32)).astype(
                    bf16
                )

            grad_keep(t).start()

    share = cols_out.shape[2]

    def to_columns(n):
        owner = lax.rem(ctx + n, group)
        block = w_out.at[
            pl.ds(pl.multiple_of(dp * share, share), share),
            pl.ds(pl.multiple_of(owner * head_cols, head_cols), head_cols),
        ]
        if n == 0:
            return pltpu.make_async_copy(block, cols_out.at[ctx, dp], cols_send.at[0])
        return copy_to(
            block, cols_out.at[ctx, dp], cols_send.at[n], cols_recv.at[n], (dp, owner)
        )

    def columns_arrive():
        to_columns(0).wait()
        for n in range(1, group):
            source = lax.rem(ctx + group - n, group)
            here = cols_out.at[source, dp]
            copy_to(here, here, cols_send.at[n], cols_recv.at[n], other).wait_recv()

    def columns_core(which):
        here = cols_out.at[:, pl.ds(2 * x + which, 1)]
        return copy_to(here, here, cols_send.at[group], cols_recv.at[group], sibling)

    def columns_x(which):
        here = cols_out.at[:, pl.ds(2 * which, 2)]
        return copy_to(here, here, cols_send.at[group + 1], cols_recv.at[group + 1], across)

    def to_head(j):
        target = lax.rem(3 * ctx + j, group)
        remote = copy_to(
            heads.at[j], heads_out.at[j], head_send.at[j], head_recv.at[j], (dp, target)
        )
        local = pltpu.make_async_copy(heads.at[j], heads_out.at[j], head_recv.at[j])
        return target == ctx, remote, local

    for n in range(group):
        to_columns(n).start()
    turn(1)
    own[0].wait()
    y_arrive(0, 0)
    forward(0)
    turn(2)
    y_arrive(0, 1)
    forward(1)
    turn(3)
    y_arrive(0, 2)
    forward(2)
    turn(4)
    y_arrive(0, 3)
    forward(3)
    turn(5)
    own[1].wait()
    y_arrive(1, 0)
    backward(0)
    turn(6)
    y_arrive(1, 1)
    backward(1)
    turn(7)
    for j in range(3):
        here, remote, local = to_head(j)
        pl.when(here)(lambda local=local: local.start())
        pl.when(jnp.logical_not(here))(lambda remote=remote: remote.start())
    columns_arrive()
    columns_core(core).start()
    y_arrive(1, 2)
    backward(2)
    columns_core(1 - core).wait_recv()
    columns_x(x).start()
    y_arrive(1, 3)
    backward(3)
    outer(0, act, g_buf)
    outer(1, pre_grad, x_mlp)
    outer_sum(0)
    outer_sum(1)

    for at_z in range(depth):
        to_other(0, at_z).wait_send()
        to_other(1, at_z).wait_send()
        for i in range(2):
            pl.when(has_above & (at_z <= z))(lambda i=i: upward(i, at_z).wait_send())
            pl.when(has_below & (at_z >= z))(lambda i=i: downward(i, at_z).wait_send())
    for j in range(3):
        here, remote, local = to_head(j)
        pl.when(here)(lambda local=local: local.wait())
        pl.when(jnp.logical_not(here))(lambda remote=remote: remote.wait_send())
        source = lax.rem(pow(3, -1, group) * (ctx + group - j), group)
        pl.when(source != ctx)(lambda remote=remote: remote.wait_recv())
    for s in range(4):
        keep(0, s, h_buf, h_out).wait()
        keep(1, s, x_attn, x_out).wait()
        keep(2, s, g_buf, g_out).wait()
        keep(3, s, part, part_out).wait()
        keep(4, s, back, back_out).wait()
    for t in range(2 * tiles):
        to_core(t).wait_send()
        grad_keep(t).wait()
    for n in range(1, group):
        to_columns(n).wait_send()
    columns_core(core).wait_send()
    columns_x(x).wait_send()
    columns_x(1 - x).wait_recv()


def layer_pass(
    group, hidden, grad, w_up, w_down, w_qkv, w_out, norms, bias_up, bias_qkv, seg_len, seg_parent
):
    rows, columns = hidden.shape
    tokens, units, head_cols = group * rows, w_up.shape[0], w_qkv.shape[0] // 3
    depth = group // RAILS
    inverse = jnp.power(10000.0, -2.0 * jnp.arange(ROT_DIM // 2, dtype=f32) / ROT_DIM)
    inverse = jnp.broadcast_to(inverse[:, None], (ROT_DIM // 2, rows))
    sems = pltpu.SemaphoreType.DMA
    shape = jax.ShapeDtypeStruct
    anywhere = pl.BlockSpec(memory_space=pl.ANY)
    vmem = pl.BlockSpec(memory_space=pltpu.VMEM)
    smem = pl.BlockSpec(memory_space=pltpu.SMEM)
    whole = shape((tokens, columns), bf16)
    half = 128
    copies = lax.axis_size("dp")
    return pl.pallas_call(
        functools.partial(layer_kernel, group),
        out_shape=(
            whole,
            whole,
            whole,
            shape((3, tokens, head_cols), bf16),
            whole,
            whole,
            shape((units, columns), bf16),
            shape((group, copies, columns // group // copies, head_cols), bf16),
            shape((4, tokens, HEAD_DIM), f32),
            shape((2, columns), f32),
            shape((1, units), f32),
        ),
        in_specs=[anywhere] * 6 + [vmem] * 4 + [smem] * 2,
        out_specs=[anywhere] * 8 + [vmem] * 3,
        scratch_shapes=[pltpu.VMEM((tokens, columns), bf16)] * 2
        + [pltpu.VMEM((units, columns), bf16)] * 2
        + [pltpu.VMEM((3 * head_cols, columns), bf16)]
        + [pltpu.VMEM((tokens, columns), bf16)] * 2
        + [pltpu.VMEM((tokens, units), bf16)] * 3
        + [pltpu.VMEM((3, tokens, head_cols), bf16)]
        + [pltpu.VMEM((tokens, columns), bf16)] * 2
        + [pltpu.VMEM((units, columns), bf16)] * 2
        + [pltpu.VMEM((units // half, half, columns), bf16)]
        + [pltpu.VMEM((tokens, 1), f32)] * 2
        + [sems((2,))]
        + [sems((2, depth))] * 6
        + [sems((3,)), sems((5, 4)), sems((units // half,)), sems((3,)), sems((3,))]
        + [sems((units // half,))] * 2
        + [sems((group + 2,))] * 2,
        compiler_params=pltpu.CompilerParams(
            collective_id=0, has_side_effects=True, vmem_limit_bytes=61 * 2**20
        ),
        name="layer_pass",
    )(hidden, grad, w_up, w_down, w_qkv, w_out, norms, bias_up, bias_qkv, inverse, seg_len, seg_parent)


def tail_kernel(group, *refs):
    pairs, arrived_in, grad_in, w_cols_in, part_in, back_in, x_in, w_qkv_in, hidden_in = refs[:9]
    tables_in, norms, mlp_sums, up_sums, local_sums, seg_len, seg_parent = refs[9:16]
    part_out, back_out, down_out, up_out, out_out, qkv_out, vectors_out = refs[16:23]
    refs = refs[23:]
    arrived, g_buf, w_cols, part, back, x_buf, w_qkv, h_buf, tables = refs[:9]
    att_grad, attended, returns, returned, y_buf, z_buf = refs[9:15]
    out_grad, qkv_grad, qkv_core, out_core, out_rows, from_x, pairs_x, key_acc, value_acc = refs[15:24]
    sums, vec_buf = refs[24:26]
    (
        load_sem,
        y_send,
        y_recv,
        up_send,
        up_recv,
        down_send,
        down_recv,
        result_sem,
        head_send,
        head_recv,
        pair_send,
        pair_recv,
        core_send,
        core_recv,
        block_send,
        block_recv,
        x_send,
        x_recv,
        keep_sem,
        done_send,
        done_recv,
        vec_send,
        vec_recv,
        sum_sem,
    ) = refs[26:]
    dp, ctx, z, y, depth = place(group)
    tokens, columns = g_buf.shape
    rows = tokens // group
    head_cols = attended.shape[1]
    heads = head_cols // HEAD_DIM
    half = qkv_core.shape[1]
    pair_tiles = pairs_x.shape[0]
    x, core = dp // 2, dp % 2
    other = (dp, z * RAILS + 1 - y)
    above = (dp, jnp.minimum(z + 1, depth - 1) * RAILS + y)
    below = (dp, jnp.maximum(z - 1, 0) * RAILS + y)
    sibling = (x * 2 + 1 - core, ctx)
    across = ((1 - x) * 2 + core, ctx)
    near = (dp, (z + 1 - 2 * (z % 2)) * RAILS + y)
    far = (dp, lax.rem(z + 2, depth) * RAILS + y)
    has_above, has_below = z < depth - 1, z > 0

    for n in range(1, group):
        signal((dp, lax.rem(ctx + n, group)))
    signal(sibling)
    signal(across)
    arrive(group + 1)

    def add(target, left, right):
        step = 32

        @pl.loop(0, target.shape[0] // step)
        def _(n):
            at = pl.ds(pl.multiple_of(n * step, step), step)
            target[at, :] = (left[at, :].astype(f32) + right[at, :].astype(f32)).astype(
                target.dtype
            )

    def pair_x(t):
        return copy_to(
            pairs.at[pl.ds(t * half, half)],
            pairs_x.at[t],
            pair_send.at[t],
            pair_recv.at[t],
            across,
        )

    for t in range(pair_tiles):
        pair_x(t).start()
    loads = [
        pltpu.make_async_copy(source, held, load_sem.at[n])
        for n, (source, held) in enumerate(
            (
                (w_cols_in, w_cols),
                (grad_in, g_buf),
                (arrived_in, arrived),
                (tables_in, tables),
                (part_in, part),
                (w_qkv_in, w_qkv),
                (back_in, back),
                (hidden_in, h_buf),
                (x_in, x_buf),
            )
        )
    ]
    for copy in loads:
        copy.start()

    wide = 512
    tall = 256
    scale = 1.0 / math.sqrt(HEAD_DIM)
    loads[0].wait()
    loads[1].wait()

    @pl.loop(0, tokens // tall)
    def _(n):
        at = pl.ds(pl.multiple_of(n * tall, tall), tall)
        att_grad[at, :] = dot_nn(g_buf[at, :], w_cols[...]).astype(bf16)

    starts, reaches = [], []
    at = jnp.int32(0)
    for n in range(seg_len.shape[1]):
        parent = seg_parent[0, n]
        grand = seg_parent[0, parent]
        starts.append(at)
        reaches.append(
            (jnp.int32(1) << n) | (jnp.int32(1) << parent) | (jnp.int32(1) << grand)
        )
        at = at + seg_len[0, n]
    loads[2].wait()
    loads[3].wait()
    slots = [lax.rem(kind * group + ctx, 3) for kind in range(3)]

    def unturn(values, at):
        return (
            values * tables[0, at, :]
            - pltpu.roll(values, HEAD_DIM - ROT_DIM // 2, 1) * tables[1, at, :]
            - pltpu.roll(values, ROT_DIM // 2, 1) * tables[2, at, :]
        )

    for m in range(heads):
        lanes = slice(m * HEAD_DIM, (m + 1) * HEAD_DIM)
        key_acc[...] = jnp.zeros_like(key_acc)
        value_acc[...] = jnp.zeros_like(value_acc)
        for n in range(tokens // tall):
            mine = pl.ds(n * tall, tall)
            seen = (n + 1) * tall
            upto = pl.ds(0, seen)
            token = n * tall + lax.broadcasted_iota(jnp.int32, (tall, 1), 0)
            key = lax.broadcasted_iota(jnp.int32, (1, seen), 1)
            reach = jnp.zeros((tall, 1), jnp.int32) + reaches[0]
            label = jnp.ones((1, seen), jnp.int32)
            for k in range(1, len(starts)):
                reach = jnp.where(token >= starts[k], reaches[k], reach)
                label = jnp.where(key >= starts[k], 1 << k, label)
            allowed = ((reach & label) != 0) & (key <= token)
            query = arrived[slots[0], mine, lanes]
            keys = arrived[slots[1], upto, lanes]
            values = arrived[slots[2], upto, lanes]
            out_grad_rows = att_grad[mine, lanes]
            scores = jnp.where(allowed, dot_nt(query, keys) * scale, masked_score)
            expo = jnp.exp(scores - jnp.max(scores, axis=1, keepdims=True))
            probs = expo * (1.0 / jnp.sum(expo, axis=1, keepdims=True))
            weights = probs.astype(bf16)
            attended[mine, lanes] = dot_nn(weights, values).astype(bf16)
            prob_grad = dot_nt(out_grad_rows, values)
            delta = jnp.sum(probs * prob_grad, axis=1, keepdims=True)
            score_grad = (probs * (prob_grad - delta)).astype(bf16)
            query_grad = dot_nn(score_grad, keys) * scale
            returns[slots[0], mine, lanes] = unturn(query_grad, mine).astype(bf16)
            key_acc[upto, :] += dot_tn(score_grad, query)
            value_acc[upto, :] += dot_tn(weights, out_grad_rows)

        for n in range(tokens // tall):
            mine = pl.ds(n * tall, tall)
            returns[slots[1], mine, lanes] = unturn(key_acc[mine, :] * scale, mine).astype(bf16)
            returns[slots[2], mine, lanes] = value_acc[mine, :].astype(bf16)

    back_step = pow(3, -1, group)

    def to_owner(j):
        owner = lax.rem(back_step * (ctx + group - j), group)
        remote = copy_to(
            returns.at[j], returned.at[j], head_send.at[j], head_recv.at[j], (dp, owner)
        )
        local = pltpu.make_async_copy(returns.at[j], returned.at[j], head_recv.at[j])
        return owner == ctx, remote, local

    for j in range(3):
        here, remote, local = to_owner(j)
        pl.when(here)(lambda local=local: local.start())
        pl.when(jnp.logical_not(here))(lambda remote=remote: remote.start())

    @pl.loop(0, group)
    def _(n):
        at = pl.ds(pl.multiple_of(n * head_cols, head_cols), head_cols)
        out_grad[n] = dot_tn(g_buf[:, at], attended[...]).astype(bf16)

    core_tiles = qkv_core.shape[0]
    out_to_core = copy_to(
        out_grad.at[:, pl.ds((1 - core) * half, half)],
        out_core,
        core_send.at[core_tiles],
        core_recv.at[core_tiles],
        sibling,
    )
    out_to_core.start()

    loads[4].wait()

    @pl.loop(0, tokens // tall)
    def _(n):
        at = pl.ds(pl.multiple_of(n * tall, tall), tall)

        @pl.loop(0, columns // wide)
        def _(m):
            cols = pl.ds(pl.multiple_of(m * wide, wide), wide)
            part[at, cols] = (
                part[at, cols].astype(f32) + dot_nt(attended[at, :], w_cols[cols, :])
            ).astype(bf16)

    out_to_core.wait_recv()

    @pl.loop(0, group)
    def _(n):
        out_core[n] = (
            out_core[n].astype(f32)
            + out_grad[n, pl.ds(pl.multiple_of(core * half, half), half), :].astype(f32)
        ).astype(bf16)

    my_cols = pl.ds(pl.multiple_of(ctx * head_cols, head_cols), head_cols)

    def out_block(n):
        owner = lax.rem(ctx + n, group)
        return copy_to(
            out_core.at[owner],
            out_rows.at[:, my_cols],
            block_send.at[n],
            block_recv.at[n],
            (dp, owner),
        )

    for n in range(1, group):
        out_block(n).start()
    own_block = pltpu.make_async_copy(out_core.at[ctx], out_rows.at[:, my_cols], block_send.at[0])
    own_block.start()

    low = z < depth // 2
    order = [
        jnp.where(low, depth - 1, 0),
        jnp.where(low, depth - 2, 1),
        jnp.where(low, 1 - z, 2 * depth - 3 - z),
        z,
    ]
    parts = (part, back)

    def chunk(i, at_z, at_y):
        return parts[i].at[pl.ds(pl.multiple_of((at_z * RAILS + at_y) * rows, rows), rows)]

    def swap(i, s):
        return copy_to(
            chunk(i, order[s], 1 - y),
            y_buf.at[i, order[s]],
            y_send.at[i, s],
            y_recv.at[i, s],
            other,
        )

    def upward(i, at):
        return copy_to(
            chunk(i, at, y), z_buf.at[i, at], up_send.at[i, at], up_recv.at[i, at], above
        )

    def downward(i, at, slot):
        return copy_to(
            chunk(i, at, y), z_buf.at[i, slot], down_send.at[i, at], down_recv.at[i, at], below
        )

    def down_slot(at, owner_z):
        return jnp.where(at == owner_z, depth, at)

    def scatter_step(i, s):
        at = order[s]
        swap(i, s).wait_recv()
        mine = chunk(i, at, y)
        add(mine, mine, y_buf.at[i, at])

        @pl.when((at >= z) & has_below)
        def _():
            upward(i, at).wait_recv()
            add(mine, mine, z_buf.at[i, at])

        @pl.when((at <= z) & has_above)
        def _():
            slot = down_slot(at, z)
            downward(i, at, slot).wait_recv()
            add(mine, mine, z_buf.at[i, slot])

        pl.when(at > z)(lambda: upward(i, at).start())
        pl.when(at < z)(lambda: downward(i, at, down_slot(at, z - 1)).start())

    results = (part_out, back_out)

    def scatter_out(i):
        return pltpu.make_async_copy(chunk(i, z, y), results[i], result_sem.at[i])

    for s in range(depth):
        swap(0, s).start()

    for j in range(3):
        here, remote, local = to_owner(j)
        pl.when(here)(lambda local=local: local.wait())
        target = lax.rem(3 * ctx + j, group)
        pl.when(target != ctx)(lambda remote=remote: remote.wait_recv())
    for n in (5, 6, 7):
        loads[n].wait()
    sums[...] = jnp.zeros_like(sums)

    @pl.loop(0, tokens // tall)
    def _(n):
        at = pl.ds(pl.multiple_of(n * tall, tall), tall)

        @pl.loop(0, columns // wide)
        def _(m):
            cols = pl.ds(pl.multiple_of(m * wide, wide), wide)
            entry = dot_nn(returned[0, at, :], w_qkv[0:head_cols, cols])
            for j in range(1, 3):
                entry += dot_nn(
                    returned[j, at, :], w_qkv[j * head_cols : (j + 1) * head_cols, cols]
                )
            normed = (h_buf[at, cols].astype(f32) - tables[3, at, 0:1]) * tables[3, at, 1:2]
            sums[0:1, cols] += jnp.sum(entry * normed, axis=0, keepdims=True)
            sums[1:2, cols] += jnp.sum(entry, axis=0, keepdims=True)
            back[at, cols] = (back[at, cols].astype(f32) + entry * norms[0:1, cols]).astype(bf16)

    stages = (sibling, other, near, far, across)

    def exchange(n):
        return copy_to(
            vec_buf.at[2 * n], vec_buf.at[2 * n + 1], vec_send.at[n], vec_recv.at[n], stages[n]
        )

    lane_cols = vec_buf.shape[2]

    def place_vector(at, values):
        for n in range(values.shape[1] // lane_cols):
            vec_buf[0, pl.ds(at + n, 1), :] = values[:, n * lane_cols : (n + 1) * lane_cols]

    vec_buf[0] = jnp.zeros(vec_buf.shape[1:], f32)
    long = columns // lane_cols
    place_vector(0, sums[0:1, :])
    place_vector(long, sums[1:2, :])
    place_vector(2 * long, mlp_sums[0:1, :])
    place_vector(3 * long, mlp_sums[1:2, :])
    place_vector(4 * long, local_sums[...])
    each = head_cols // lane_cols
    for j in range(3):
        place_vector(
            5 * long + (3 * ctx + j) * each,
            jnp.sum(returned[j].astype(f32), axis=0, keepdims=True),
        )
    place_vector(
        5 * long + 3 * group * each + ctx * (up_sums.shape[1] // lane_cols), up_sums[...]
    )
    exchange(0).start()

    def vector_step(n):
        exchange(n).wait_recv()
        total = vec_buf[2 * n] + vec_buf[2 * n + 1]
        if n + 1 < len(stages):
            vec_buf[2 * n + 2] = total
            exchange(n + 1).start()
        else:
            vectors_out[...] = total

    vector_step(0)
    for s in range(depth):
        swap(1, s).start()

    loads[8].wait()

    def qkv_half(t, which):
        start = pl.multiple_of(t * 2 * half + which * half, half)
        return qkv_grad.at[pl.ds(start, half)]

    def to_core(t):
        return copy_to(
            qkv_half(t, 1 - core), qkv_core.at[t], core_send.at[t], core_recv.at[t], sibling
        )

    for t in range(core_tiles):

        @pl.loop(0, columns // (2 * wide))
        def _(m):
            cols = pl.ds(pl.multiple_of(m * 2 * wide, 2 * wide), 2 * wide)
            qkv_grad[pl.ds(t * 2 * half, 2 * half), cols] = dot_tn(
                returned[t], x_buf[:, cols]
            ).astype(bf16)

        to_core(t).start()

    def across_x(t):
        source = qkv_half(t, core) if t < core_tiles else out_rows
        return copy_to(source, from_x.at[t], x_send.at[t], x_recv.at[t], across)

    spots = (
        [(down_out, 2 * half * t) for t in range(pair_tiles // 2)]
        + [(up_out, 2 * half * t) for t in range(pair_tiles // 2)]
        + [(qkv_out, 2 * half * t) for t in range(core_tiles)]
        + [(out_out, 0)]
    )
    again = pltpu.make_async_copy(pairs, g_buf, sum_sem.at[0])
    again.start()

    def total_of(t):
        return pairs_x.at[t] if t < pair_tiles else from_x.at[t - pair_tiles]

    def spot(t, which):
        array, first = spots[t]
        return array.at[pl.ds(pl.multiple_of(first + which * half, half), half)]

    def keep(t):
        return pltpu.make_async_copy(total_of(t), spot(t, core), keep_sem.at[t])

    def finish(t, which):
        return copy_to(total_of(t), spot(t, which), done_send.at[t], done_recv.at[t], sibling)

    def x_sum(t):
        total = total_of(t)
        if t < pair_tiles:
            pair_x(t).wait_recv()
            add(total, total, g_buf.at[pl.ds(t * half, half)])
        else:
            n = t - pair_tiles
            across_x(n).wait_recv()
            add(total, total, qkv_half(n, core) if n < core_tiles else out_rows)
        keep(t).start()
        finish(t, core).start()

    for t in range(core_tiles):
        to_core(t).wait_recv()
        mine = qkv_half(t, core)
        add(mine, mine, qkv_core.at[t])
        across_x(t).start()
    own_block.wait()
    for n in range(1, group):
        source = lax.rem(ctx + group - n, group)
        theirs = pl.ds(pl.multiple_of(source * head_cols, head_cols), head_cols)
        copy_to(
            out_core.at[ctx], out_rows.at[:, theirs], block_send.at[n], block_recv.at[n], other
        ).wait_recv()
    again.wait()
    for s in range(depth):
        scatter_step(0, s)
        x_sum(2 * s)
        x_sum(2 * s + 1)
    scatter_out(0).start()
    vector_step(1)
    for s in range(depth):
        scatter_step(1, s)
        if s < 2:
            vector_step(s + 2)
        if s == 1:
            across_x(core_tiles).start()
        x_sum(pair_tiles + s)
    vector_step(4)
    scatter_out(1).start()

    for j in range(3):
        here, remote, local = to_owner(j)
        pl.when(jnp.logical_not(here))(lambda remote=remote: remote.wait_send())
    for n in range(1, group):
        out_block(n).wait_send()
    out_to_core.wait_send()
    for t in range(core_tiles):
        to_core(t).wait_send()
    for t in range(core_tiles + 1):
        across_x(t).wait_send()
    for t in range(pair_tiles):
        pair_x(t).wait_send()
    for t in range(len(spots)):
        keep(t).wait()
        finish(t, core).wait_send()
        finish(t, 1 - core).wait_recv()
    for n in range(len(stages)):
        exchange(n).wait_send()
    for i in range(2):
        scatter_out(i).wait()
        for s in range(depth):
            swap(i, s).wait_send()
            at = order[s]
            pl.when(at > z)(lambda i=i, at=at: upward(i, at).wait_send())
            pl.when(at < z)(
                lambda i=i, at=at: downward(i, at, down_slot(at, z - 1)).wait_send()
            )


def tail_pass(
    group,
    pairs,
    arrived,
    grad_all,
    w_cols,
    part,
    back,
    x_attn,
    w_qkv,
    hidden_all,
    tables,
    norms,
    mlp_sums,
    up_sums,
    local_sums,
    seg_len,
    seg_parent,
):
    tokens, columns = hidden_all.shape
    depth = group // RAILS
    rows = tokens // group
    head_cols = arrived.shape[2]
    units = up_sums.shape[1]
    half = 128
    pair_tiles = pairs.shape[0] // half
    core_tiles = w_qkv.shape[0] // (2 * half)
    lane_cols = 256
    vectors = (5 * columns + 3 * columns + group * units) // lane_cols
    sems = pltpu.SemaphoreType.DMA
    shape = jax.ShapeDtypeStruct
    vmem = pltpu.VMEM
    anywhere = pl.BlockSpec(memory_space=pl.ANY)
    small = pl.BlockSpec(memory_space=pltpu.VMEM)
    smem = pl.BlockSpec(memory_space=pltpu.SMEM)
    whole = vmem((tokens, columns), bf16)
    every = pair_tiles + core_tiles + 1
    return pl.pallas_call(
        functools.partial(tail_kernel, group),
        out_shape=(
            shape((rows, columns), bf16),
            shape((rows, columns), bf16),
            shape((units, columns), bf16),
            shape((units, columns), bf16),
            shape((2 * half, columns), bf16),
            shape(w_qkv.shape, bf16),
            shape((vectors, lane_cols), f32),
        ),
        in_specs=[anywhere] * 10 + [small] * 4 + [smem] * 2,
        out_specs=[anywhere] * 6 + [small],
        scratch_shapes=[
            vmem(arrived.shape, bf16),
            whole,
            vmem(w_cols.shape, bf16),
            whole,
            whole,
            whole,
            vmem(w_qkv.shape, bf16),
            whole,
            vmem(tables.shape, f32),
            vmem((tokens, head_cols), bf16),
            vmem((tokens, head_cols), bf16),
            vmem(arrived.shape, bf16),
            vmem(arrived.shape, bf16),
            vmem((2, depth, rows, columns), bf16),
            vmem((2, depth + 1, rows, columns), bf16),
            vmem((group, 2 * half, head_cols), bf16),
            vmem(w_qkv.shape, bf16),
            vmem((core_tiles, half, columns), bf16),
            vmem((group, half, head_cols), bf16),
            vmem((half, columns), bf16),
            vmem((core_tiles + 1, half, columns), bf16),
            vmem((pair_tiles, half, columns), bf16),
            vmem((tokens, HEAD_DIM), f32),
            vmem((tokens, HEAD_DIM), f32),
            vmem((2, columns), f32),
            vmem((10, vectors, lane_cols), f32),
            sems((9,)),
        ]
        + [sems((2, depth))] * 6
        + [sems((2,)), sems((3,)), sems((3,)), sems((pair_tiles,)), sems((pair_tiles,))]
        + [sems((core_tiles + 1,))] * 2
        + [sems((group,))] * 2
        + [sems((core_tiles + 1,))] * 2
        + [sems((every,))] * 3
        + [sems((5,))] * 2
        + [sems((1,))],
        compiler_params=pltpu.CompilerParams(
            collective_id=1, has_side_effects=True, vmem_limit_bytes=61 * 2**20
        ),
        name="tail_pass",
    )(
        pairs,
        arrived,
        grad_all,
        w_cols,
        part,
        back,
        x_attn,
        w_qkv,
        hidden_all,
        tables,
        norms,
        mlp_sums,
        up_sums,
        local_sums,
        seg_len,
        seg_parent,
    )


def body(
    hidden_in,
    grad_out,
    seg_len,
    seg_parent,
    gain_attn,
    shift_attn,
    w_qkv,
    bias_qkv,
    w_out,
    bias_out,
    gain_mlp,
    shift_mlp,
    w_up,
    bias_up,
    w_down,
    bias_down,
):
    group = lax.axis_size("ctx")
    me = lax.axis_index("ctx")
    local_rows = hidden_in.shape[1]
    tokens = local_rows * group
    head_count = HEADS // group
    head_cols = head_count * HEAD_DIM
    norms = jnp.stack([gain_attn, shift_attn, gain_mlp, shift_mlp]).astype(f32)
    up_bias = lax.dynamic_slice_in_dim(bias_up, me * w_up.shape[0], w_up.shape[0])
    qkv_bias = lax.dynamic_slice_in_dim(bias_qkv, me * 3 * head_cols, 3 * head_cols)
    (
        hidden_all,
        grad_all,
        x_attn,
        arrived,
        mlp_part,
        mlp_back,
        pairs,
        w_cols,
        tables,
        mlp_sums,
        up_sums,
    ) = layer_pass(
        group,
        hidden_in[0],
        grad_out[0],
        w_up,
        w_down,
        w_qkv,
        w_out,
        norms,
        up_bias.astype(f32)[None],
        qkv_bias.astype(f32)[None],
        seg_len,
        seg_parent,
    )
    grad_f = grad_out[0].astype(f32)
    summed, w_sum, down_grad, up_grad, out_grad, qkv_grad, vectors = tail_pass(
        group,
        pairs,
        arrived,
        grad_all,
        w_cols.reshape(D, head_cols),
        mlp_part,
        mlp_back,
        x_attn,
        w_qkv,
        hidden_all,
        tables,
        norms,
        mlp_sums,
        up_sums,
        jnp.sum(grad_f, axis=0)[None],
        seg_len,
        seg_parent,
    )
    vectors = vectors.reshape(-1)
    w_sum = w_sum.astype(f32)
    hidden_out = (
        hidden_in[0].astype(f32) + summed.astype(f32) + bias_out.astype(f32) + bias_down.astype(f32)
    ).astype(bf16)
    mine = lax.dynamic_slice_in_dim(tables[3], me * local_rows, local_rows)
    my_rstd = mine[:, 1:2]
    my_normed = (hidden_in[0].astype(f32) - mine[:, :1]) * my_rstd
    grad_in = (
        grad_f
        + (
            w_sum
            - jnp.mean(w_sum, axis=-1, keepdims=True)
            - my_normed * jnp.mean(w_sum * my_normed, axis=-1, keepdims=True)
        )
        * my_rstd
    )

    cuts = [D, D, D, D, D, 3 * D, FF]
    ends = [sum(cuts[: i + 1]) for i in range(len(cuts))]
    (
        gain_grad_a,
        shift_grad_a,
        gain_grad_m,
        shift_grad_m,
        out_bias_grad,
        qkv_bias_grad,
        up_bias_grad,
    ) = [vectors[end - cut : end] for cut, end in zip(cuts, ends)]
    return (
        hidden_out[None],
        grad_in[None],
        gain_grad_a,
        shift_grad_a,
        qkv_grad.astype(f32),
        qkv_bias_grad,
        out_grad.astype(f32),
        out_bias_grad,
        gain_grad_m,
        shift_grad_m,
        up_grad.astype(f32),
        up_bias_grad,
        down_grad.astype(f32),
        out_bias_grad,
    )


block_limit = 512


def tree_tables(seg_len, seg_parent):
    seg_count = seg_len.shape[0]
    labels = jnp.arange(seg_count, dtype=jnp.int32)
    earlier = labels[:, None] > labels[None, :]
    seg_starts = jnp.sum(jnp.where(earlier, seg_len[None, :], 0), axis=1)
    seg_ends = seg_starts + seg_len
    parent_hit = seg_parent[:, None] == labels[None, :]
    grand_parent = jnp.sum(jnp.where(parent_hit, seg_parent[None, :], 0), axis=1)
    itself = labels[:, None] == labels[None, :]
    ancestor = itself | parent_hit | (grand_parent[:, None] == labels[None, :])
    path_start = jnp.sum(jnp.where(ancestor & jnp.logical_not(itself), seg_len[None, :], 0), axis=1)
    return (seg_ends, seg_starts, ancestor, path_start)


def rotary_tables(path_pos):
    half_dim = ROT_DIM // 2
    inverse = jnp.power(10000.0, -2.0 * jnp.arange(half_dim, dtype=jnp.float32) / ROT_DIM)
    angles = path_pos.astype(jnp.float32)[:, None] * inverse[None, :]
    angles = jnp.concatenate([angles, angles], axis=1)
    return (jnp.cos(angles), jnp.sin(angles))


def rotate(head_values, cosine, sine):
    half_dim = ROT_DIM // 2
    turned = head_values[..., :ROT_DIM]
    swapped = jnp.concatenate([-turned[..., half_dim:], turned[..., :half_dim]], axis=-1)
    mixed = turned * cosine[:, None, :] + swapped * sine[:, None, :]
    return jnp.concatenate([mixed, head_values[..., ROT_DIM:]], axis=-1)


def gelu_slope(pre_act):
    normal_cdf = 0.5 * (1.0 + lax.erf(pre_act / math.sqrt(2.0)))
    return normal_cdf + pre_act * jnp.exp(-0.5 * pre_act * pre_act) / math.sqrt(2.0 * math.pi)


def layer_norm(values, gain_vec, shift_vec):
    average = jnp.mean(values, axis=-1, keepdims=True)
    centred = values - average
    spread = jnp.mean(centred * centred, axis=-1, keepdims=True)
    return centred * lax.rsqrt(spread + norm_eps) * gain_vec + shift_vec


def segment_hot(row_ids, seg_ends):
    seg_index = jnp.sum((row_ids[:, None] >= seg_ends[None, :]).astype(jnp.int32), axis=1)
    labels = jnp.arange(seg_ends.shape[0], dtype=jnp.int32)
    return (seg_index[:, None] == labels[None, :]).astype(jnp.float32)


def row_lookup(row_ids, seg_ends, ancestor_f):
    row_hot = segment_hot(row_ids, seg_ends)
    return (row_hot, jnp.dot(row_hot, ancestor_f))


def permitted(query_ids, query_reach, key_ids, key_hot):
    linked = jnp.dot(query_reach, key_hot.T) > 0.5
    return linked & (key_ids[None, :] <= query_ids[:, None])


def inner_block(row_count):
    block_rows = row_count
    while block_rows > block_limit and block_rows % 2 == 0:
        block_rows = block_rows // 2
    return block_rows


def gather_body(
    hidden_in,
    grad_out,
    seg_len,
    seg_parent,
    gain_attn,
    shift_attn,
    w_qkv,
    bias_qkv,
    w_out,
    bias_out,
    gain_mlp,
    shift_mlp,
    w_up,
    bias_up,
    w_down,
    bias_down,
):
    local_rows = hidden_in.shape[1]
    scale_factor = 1.0 / math.sqrt(HEAD_DIM)
    head_shape = (local_rows, HEADS, HEAD_DIM)
    seg_ends, seg_starts, ancestor, path_start = tree_tables(seg_len[0], seg_parent[0])
    ancestor_f = ancestor.astype(jnp.float32)
    my_ids = lax.axis_index("ctx") * local_rows + jnp.arange(local_rows, dtype=jnp.int32)
    my_hot, my_reach = row_lookup(my_ids, seg_ends, ancestor_f)
    shift_table = path_start - seg_starts
    path_pos = my_ids + jnp.sum(my_hot.astype(jnp.int32) * shift_table[None, :], axis=1)
    cosine, sine = rotary_tables(path_pos)
    inputs_f = hidden_in[0].astype(jnp.float32)
    gain_a = gain_attn.astype(jnp.float32)
    shift_a = shift_attn.astype(jnp.float32)
    gain_m = gain_mlp.astype(jnp.float32)
    shift_m = shift_mlp.astype(jnp.float32)
    bias_up_f = bias_up.astype(jnp.float32)
    x_attn = layer_norm(inputs_f, gain_a, shift_a).astype(jnp.bfloat16)
    x_mlp = layer_norm(inputs_f, gain_m, shift_m).astype(jnp.bfloat16)
    qkv = jnp.einsum(
        "td,nd->tn",
        x_attn,
        lax.all_gather(w_qkv, "ctx", axis=0, tiled=True),
        preferred_element_type=jnp.float32,
    ) + bias_qkv.astype(jnp.float32)
    queries = rotate(qkv[:, :D].reshape(head_shape), cosine, sine).astype(jnp.bfloat16)
    keys_heads = rotate(qkv[:, D : 2 * D].reshape(head_shape), cosine, sine).astype(jnp.bfloat16)
    values_flat = qkv[:, 2 * D :].astype(jnp.bfloat16)
    values_heads = values_flat.reshape(head_shape)
    keys_flat = keys_heads.reshape(local_rows, D)
    queries_flat = queries.reshape(local_rows, D)

    def split_blocks(shard_pieces):
        row_count = shard_pieces[0].shape[0]
        block_rows = inner_block(row_count)
        block_count = row_count // block_rows
        shaped = tuple(
            (member.reshape(block_count, block_rows, HEADS, HEAD_DIM) for member in shard_pieces)
        )
        starts = block_rows * jnp.arange(block_count, dtype=jnp.int32)
        return shaped + (starts,)

    def attend_block(fold_state, block_items):
        key_block, value_block, block_start = block_items
        block_rows = key_block.shape[0]
        key_ids = block_start + jnp.arange(block_rows, dtype=jnp.int32)
        allowed = permitted(my_ids, my_reach, key_ids, segment_hot(key_ids, seg_ends))
        row_top, row_total, partial_value = fold_state
        scores = (
            jnp.einsum("qhd,khd->qhk", queries, key_block, preferred_element_type=jnp.float32)
            * scale_factor
        )
        scores = jnp.where(allowed[:, None, :], scores, masked_score)
        new_top = jnp.maximum(row_top, jnp.max(scores, axis=-1))
        factor = jnp.exp(row_top - new_top)
        weights = jnp.exp(scores - new_top[:, :, None])
        row_total = row_total * factor + jnp.sum(weights, axis=-1)
        partial_value = partial_value * factor[:, :, None] + jnp.einsum(
            "qhk,khd->qhd",
            weights.astype(jnp.bfloat16),
            value_block,
            preferred_element_type=jnp.float32,
        )
        fold_state = (new_top, row_total, partial_value)
        return (fold_state, None)

    start_state = (
        jnp.full((local_rows, HEADS), masked_score, jnp.float32),
        jnp.zeros((local_rows, HEADS), jnp.float32),
        jnp.zeros(head_shape, jnp.float32),
    )
    row_top, row_total, partial_value = lax.scan(
        attend_block,
        start_state,
        split_blocks(
            (
                lax.all_gather(keys_flat, "ctx", axis=0, tiled=True),
                lax.all_gather(values_flat, "ctx", axis=0, tiled=True),
            )
        ),
    )[0]
    log_total = row_top + jnp.log(row_total)
    attended_f = partial_value / row_total[:, :, None]
    attended = attended_f.reshape(local_rows, D).astype(jnp.bfloat16)
    attn_proj = jnp.einsum(
        "td,nd->tn",
        attended,
        lax.all_gather(w_out, "ctx", axis=0, tiled=True),
        preferred_element_type=jnp.float32,
    )

    def mlp_pre(up_rows):
        return (
            jnp.einsum("td,nd->tn", x_mlp, up_rows, preferred_element_type=jnp.float32) + bias_up_f
        )

    up_rows = lax.all_gather(w_up, "ctx", axis=0, tiled=True)
    down_rows = lax.all_gather(w_down, "ctx", axis=0, tiled=True)
    activated = jax.nn.gelu(mlp_pre(up_rows), approximate=False).astype(jnp.bfloat16)
    mlp_sum = jnp.dot(activated, down_rows, preferred_element_type=jnp.float32)
    bias_out_f = bias_out.astype(jnp.float32)
    bias_down_f = bias_down.astype(jnp.float32)
    hidden_out = (inputs_f + attn_proj + bias_out_f + mlp_sum + bias_down_f).astype(jnp.bfloat16)
    grad_b = grad_out[0]
    grad_f = grad_b.astype(jnp.float32)
    up_rows = lax.all_gather(w_up, "ctx", axis=0, tiled=True)
    down_rows = lax.all_gather(w_down, "ctx", axis=0, tiled=True)
    pre_act = mlp_pre(up_rows)
    activated = jax.nn.gelu(pre_act, approximate=False).astype(jnp.bfloat16)
    act_grad = jnp.einsum("td,nd->tn", grad_b, down_rows, preferred_element_type=jnp.float32)
    pre_grad = (act_grad * gelu_slope(pre_act)).astype(jnp.bfloat16)
    input_grad = jnp.dot(pre_grad, up_rows, preferred_element_type=jnp.float32)
    act_all = activated
    pre_grad_all = pre_grad
    act_all, pre_grad_all, mlp_in_grad = (act_all, pre_grad_all, input_grad)
    attended_grad = jnp.dot(
        grad_b, lax.all_gather(w_out, "ctx", axis=0, tiled=True), preferred_element_type=jnp.float32
    ).astype(jnp.bfloat16)
    attended_grad_heads = attended_grad.reshape(head_shape)
    row_delta = jnp.sum(attended_grad_heads.astype(jnp.float32) * attended_f, axis=-1)
    all_log_total, all_delta = (
        lax.all_gather(log_total, "ctx", axis=0, tiled=True),
        lax.all_gather(row_delta, "ctx", axis=0, tiled=True),
    )

    def back_block(fold_state, block_items):
        key_block, value_block, query_block, grad_block, block_start = block_items
        block_rows = key_block.shape[0]
        other_ids = block_start + jnp.arange(block_rows, dtype=jnp.int32)
        other_hot, other_reach = row_lookup(other_ids, seg_ends, ancestor_f)
        allowed_in = permitted(my_ids, my_reach, other_ids, other_hot)
        allowed_out = permitted(other_ids, other_reach, my_ids, my_hot)
        other_log = lax.dynamic_slice_in_dim(all_log_total, block_start, block_rows, 0)
        other_delta = lax.dynamic_slice_in_dim(all_delta, block_start, block_rows, 0)
        query_grad, key_grad, value_grad = fold_state
        scores = (
            jnp.einsum("qhd,khd->qhk", queries, key_block, preferred_element_type=jnp.float32)
            * scale_factor
        )
        scores = jnp.where(allowed_in[:, None, :], scores, masked_score)
        prob_mass = jnp.exp(scores - log_total[:, :, None])
        prob_grad = jnp.einsum(
            "qhd,khd->qhk", attended_grad_heads, value_block, preferred_element_type=jnp.float32
        )
        score_grad = (prob_mass * (prob_grad - row_delta[:, :, None])).astype(jnp.bfloat16)
        query_grad = (
            query_grad
            + jnp.einsum("qhk,khd->qhd", score_grad, key_block, preferred_element_type=jnp.float32)
            * scale_factor
        )
        outgoing_key_grad = key_grad
        outgoing_value_grad = value_grad
        scores = (
            jnp.einsum("qhd,khd->qhk", query_block, keys_heads, preferred_element_type=jnp.float32)
            * scale_factor
        )
        scores = jnp.where(allowed_out[:, None, :], scores, masked_score)
        prob_mass = jnp.exp(scores - other_log[:, :, None])
        outgoing_value_grad = outgoing_value_grad + jnp.einsum(
            "qhk,qhd->khd",
            prob_mass.astype(jnp.bfloat16),
            grad_block,
            preferred_element_type=jnp.float32,
        )
        prob_grad = jnp.einsum(
            "qhd,khd->qhk", grad_block, values_heads, preferred_element_type=jnp.float32
        )
        score_grad = (prob_mass * (prob_grad - other_delta[:, :, None])).astype(jnp.bfloat16)
        outgoing_key_grad = (
            outgoing_key_grad
            + jnp.einsum(
                "qhk,qhd->khd", score_grad, query_block, preferred_element_type=jnp.float32
            )
            * scale_factor
        )
        fold_state = (query_grad, outgoing_key_grad, outgoing_value_grad)
        return (fold_state, None)

    zero_heads = jnp.zeros(head_shape, jnp.float32)
    query_grad, key_grad, value_grad = lax.scan(
        back_block,
        (zero_heads, zero_heads, zero_heads),
        split_blocks(
            (
                lax.all_gather(keys_flat, "ctx", axis=0, tiled=True),
                lax.all_gather(values_flat, "ctx", axis=0, tiled=True),
                lax.all_gather(queries_flat, "ctx", axis=0, tiled=True),
                lax.all_gather(attended_grad, "ctx", axis=0, tiled=True),
            )
        ),
    )[0]

    def turn(head_values):
        return rotate(head_values, cosine, sine)

    unturn = jax.vjp(turn, zero_heads)[1]
    qkv_grad = jnp.concatenate(
        [
            unturn(query_grad)[0].reshape(local_rows, D),
            unturn(key_grad)[0].reshape(local_rows, D),
            value_grad.reshape(local_rows, D),
        ],
        axis=1,
    ).astype(jnp.bfloat16)
    attn_in_grad = jnp.dot(
        qkv_grad,
        lax.all_gather(w_qkv, "ctx", axis=0, tiled=True),
        preferred_element_type=jnp.float32,
    )
    pull_attn = jax.vjp(layer_norm, inputs_f, gain_a, shift_a)[1]
    input_part_a, gain_grad_a, shift_grad_a = pull_attn(attn_in_grad)
    pull_mlp = jax.vjp(layer_norm, inputs_f, gain_m, shift_m)[1]
    input_part_m, gain_grad_m, shift_grad_m = pull_mlp(mlp_in_grad)
    grad_in = (grad_f + input_part_a + input_part_m)[None]
    vector_sums = lax.psum(
        (
            gain_grad_a,
            shift_grad_a,
            gain_grad_m,
            shift_grad_m,
            jnp.sum(qkv_grad, axis=0, dtype=jnp.float32),
            jnp.sum(grad_f, axis=0),
            jnp.sum(pre_grad_all, axis=0, dtype=jnp.float32),
        ),
        ("dp", "ctx"),
    )
    group_count = lax.axis_size("ctx")
    section_rows = (3 * D // group_count, D // group_count, FF // group_count, FF // group_count)
    term_sources = (
        (qkv_grad, x_attn),
        (grad_b, attended),
        (pre_grad_all, x_mlp),
        (act_all, grad_b),
    )
    owner_rows = sum(section_rows)
    blocks = jnp.arange(owner_rows * lax.axis_size("ctx") // owner_rows, dtype=jnp.int32)
    parts_list = []
    for (column_source, other_side), full_rows in zip(term_sources, section_rows):
        sub_rows = full_rows // 1
        column_ids = (
            blocks[:, None] * sub_rows + jnp.arange(sub_rows, dtype=jnp.int32)[None, :]
        ).reshape(-1)
        columns = jnp.take(column_source, column_ids, axis=1)
        block_term = jnp.einsum(
            "tr,td->rd", columns, other_side, preferred_element_type=jnp.float32
        )
        parts_list.append(block_term.reshape(blocks.shape[0], sub_rows, D))
    owned_term = lax.psum_scatter(
        jnp.concatenate(parts_list, axis=1).reshape(-1, D).astype(jnp.bfloat16),
        "ctx",
        scatter_dimension=0,
        tiled=True,
    ).astype(jnp.float32)
    cut_a = section_rows[0]
    cut_b = cut_a + section_rows[1]
    cut_c = cut_b + section_rows[2]
    weight_grads = (
        lax.psum(owned_term[:cut_a].astype(jnp.bfloat16), "dp").astype(jnp.float32),
        lax.psum(owned_term[cut_a:cut_b].astype(jnp.bfloat16), "dp").astype(jnp.float32),
        lax.psum(owned_term[cut_b:cut_c].astype(jnp.bfloat16), "dp").astype(jnp.float32),
        lax.psum(owned_term[cut_c:].astype(jnp.bfloat16), "dp").astype(jnp.float32),
    )
    return (
        hidden_out[None],
        grad_in,
        vector_sums[0],
        vector_sums[1],
        weight_grads[0],
        vector_sums[4],
        weight_grads[1],
        vector_sums[5],
        vector_sums[2],
        vector_sums[3],
        weight_grads[2],
        vector_sums[6],
        weight_grads[3],
        vector_sums[5],
    )


def solution(mesh):
    token = P("dp", "ctx", None)
    rows = P("ctx", None)
    return jax.shard_map(
        body if HEADS % mesh.shape["ctx"] == 0 else gather_body,
        mesh=mesh,
        in_specs=(
            token,
            token,
            P("dp", None),
            P("dp", None),
            P(),
            P(),
            rows,
            P(),
            rows,
            P(),
            P(),
            P(),
            rows,
            P(),
            rows,
            P(),
        ),
        out_specs=(
            token,
            token,
            P(),
            P(),
            rows,
            P(),
            rows,
            P(),
            P(),
            P(),
            rows,
            P(),
            rows,
            P(),
        ),
        check_vma=False,
    )
```

profile of v0, /device:TPU:13, one launch (start us, length us, event | category | flops | bytes accessed | tf_op | source)
XLA Modules:
  0.0 318.3 jit_solution(14667702143935335256)
XLA Ops:
  0.6 0.8 dynamic-slice_convert_fusion
  1.4 0.6 reshape.57.refs_8_
  2.0 1.3 dynamic-slice_convert_fusion.1
  3.3 0.7 stack.15
  4.0 0.7 stack.16
  4.7 0.7 stack.17
  5.4 0.7 stack.18
  6.0 0.7 maximum_convert_fusion.refs_6_.refs_10_
  6.7 0.7 broadcast_in_dim.33.refs_9_
  7.4 0.0 copy-start.1
  7.4 135.6 %layer_pass.1 = (bf16[1024,2048]{1,0:T(8,128)(2,1)}, bf16[1024,2048]{1,0:T(8,128)(2,1)}, bf16[1024,2048]{1,0:T(8,128)(2,1)}, bf16[3,1024,256]{2,1,0:T(8,128)(2,1...) custom-call(bf16[128,2048]{1,0:T(8,128)(2,1)} %bitcast.37, ...), custom_call_target="tpu_custom_call" | custom-call | tf_op jit(solution)/shard_map/layer_pass/pallas_call | solution.py:488
  143.0 0.0 copy-done.1
  143.0 0.7 convert_reduce_fusion.1
  143.7 147.5 %tail_pass.1 = (bf16[128,2048]{1,0:T(8,128)(2,1)}, bf16[128,2048]{1,0:T(8,128)(2,1)}, bf16[1024,2048]{1,0:T(8,128)(2,1)}, bf16[1024,2048]{1,0:T(8,128)(2,1)}, bf...) custom-call(bf16[1024,2048]{1,0:T(8,128)(2,1)} %get-tuple-element.32.refs_0_, ...), custom_call_target="tpu_custom_call" | custom-call | tf_op jit(solution)/shard_map/tail_pass/pallas_call | solution.py:1051
  291.2 0.0 copy-start.2
  291.2 6.8 %convert_element_type.49 = f32[1024,2048]{1,0:T(8,128)} convert(bf16[1024,2048]{1,0:T(8,128)(2,1)} %get-tuple-element.48) | non-fusion elementwise | flops 2097152 | bytes 12582912 | tf_op jit(solution)/shard_map/convert_element_type | solution.py:1238
  298.1 0.0 copy-done.2
  298.1 0.0 copy-start.3
  298.1 4.4 %convert_element_type.50 = f32[1024,2048]{1,0:T(8,128)} convert(bf16[1024,2048]{1,0:T(8,128)(2,1)S(1)} %copy-done.2) | non-fusion elementwise | flops 2097152 | bytes 12582912 | tf_op jit(solution)/shard_map/convert_element_type | solution.py:1240
  302.5 0.0 copy-done.3
  302.5 0.0 copy-start
  302.5 0.0 copy-start.4
  302.5 0.0 copy-start.8
  302.5 0.0 copy-start.9
  302.5 3.5 %convert_element_type.47 = f32[768,2048]{1,0:T(8,128)} convert(bf16[768,2048]{1,0:T(8,128)(2,1)S(1)} %copy-done.3) | non-fusion elementwise | flops 1572864 | bytes 9437184 | tf_op jit(solution)/shard_map/convert_element_type | solution.py:1232
  306.1 0.0 copy-start.5
  306.1 2.0 slice.51
  308.0 0.0 copy-start.6
  308.0 0.9 dynamic-slice_bitcast_fusion
  308.9 0.2 slice_reduce_fusion.1
  309.1 0.0 copy-done
  309.1 0.0 copy-done.4
  309.1 0.4 convert_reduce_fusion
  309.5 0.0 copy-done.8
  309.5 0.0 copy-done.9
  309.6 2.9 fusion.7
  312.4 0.0 copy-done.5
  312.4 1.6 convert_element_type.48
  314.0 0.0 copy-done.6
  314.0 0.6 copy.36
  314.6 0.0 copy-start.7
  314.7 0.6 copy.31
  315.3 0.6 copy.34
  315.9 0.6 copy.35
  316.5 0.6 copy.30
  317.1 0.6 copy.32
  317.7 0.6 copy.38
  318.3 0.0 copy-done.7
  (8 shorter events, 0.0 us)
Async XLA Ops:
  7.4 135.6 %copy-start.1 = (bf16[1,128,2048]{2,1,0:T(8,128)(2,1)S(1)}, bf16[1,128,2048]{2,1,0:T(8,128)(2,1)}, u32[]{:S(2)}) copy-start(bf16[1,128,2048]{2,1,0:T(8,128)(2,1)} %param.17) | copy-start | bytes 1572868
  291.2 6.8 %copy-start.2 = (bf16[1024,2048]{1,0:T(8,128)(2,1)S(1)}, bf16[1024,2048]{1,0:T(8,128)(2,1)}, u32[]{:S(2)}) copy-start(bf16[1024,2048]{1,0:T(8,128)(2,1)} %get-tuple-element.49) | copy-start | bytes 12582916
  298.1 4.5 %copy-start.3 = (bf16[768,2048]{1,0:T(8,128)(2,1)S(1)}, bf16[768,2048]{1,0:T(8,128)(2,1)}, u32[]{:S(2)}) copy-start(bf16[768,2048]{1,0:T(8,128)(2,1)} %get-tuple-element.46) | copy-start | bytes 9437188
  302.5 6.6 %copy-start = (bf16[1,128,2048]{2,1,0:T(8,128)(2,1)S(1)}, bf16[1,128,2048]{2,1,0:T(8,128)(2,1)}, u32[]{:S(2)}) copy-start(bf16[1,128,2048]{2,1,0:T(8,128)(2,1)} %param.16) | copy-start | bytes 1572868
  302.5 6.6 %copy-start.4 = (bf16[128,2048]{1,0:T(8,128)(2,1)S(1)}, bf16[128,2048]{1,0:T(8,128)(2,1)}, u32[]{:S(2)}) copy-start(bf16[128,2048]{1,0:T(8,128)(2,1)} %get-tuple-element.44) | copy-start | bytes 1572868
  302.5 7.0 %copy-start.8 = (bf16[2048]{0:T(1024)(128)(2,1)S(1)}, bf16[2048]{0:T(1024)(128)(2,1)}, u32[]{:S(2)}) copy-start(bf16[2048]{0:T(1024)(128)(2,1)} %param.25) | copy-start | bytes 12292
  302.5 7.0 %copy-start.9 = (bf16[2048]{0:T(1024)(128)(2,1)S(1)}, bf16[2048]{0:T(1024)(128)(2,1)}, u32[]{:S(2)}) copy-start(bf16[2048]{0:T(1024)(128)(2,1)} %param.31) | copy-start | bytes 12292
  306.1 6.3 %copy-start.5 = (bf16[256,2048]{1,0:T(8,128)(2,1)S(1)}, bf16[256,2048]{1,0:T(8,128)(2,1)}, u32[]{:S(2)}) copy-start(bf16[256,2048]{1,0:T(8,128)(2,1)} %get-tuple-element.47) | copy-start | bytes 3145732
  308.0 6.0 %copy-start.6 = (f32[96,256]{1,0:T(8,128)S(1)}, f32[96,256]{1,0:T(8,128)}, u32[]{:S(2)}) copy-start(f32[96,256]{1,0:T(8,128)} %get-tuple-element.45) | copy-start | bytes 294916
  314.6 3.7 %copy-start.7 = (f32[1,2,8,128]{3,1,2,0:T(2,128)}, f32[1,2,8,128]{3,1,2,0:T(2,128)S(1)}, u32[]{:S(2)}) copy-start(f32[1,2,8,128]{3,1,2,0:T(2,128)S(1)} %copy.33) | copy-start | bytes 24580
where the time goes:
time: 321 us; the launch traced here: 318 us
  Pallas kernels  283 us (88%)
  other arithmetic  23 us (7%)
  local copies, waits for them, and re-layouts  11.4 us (4%)
    pallas_call x1, Pallas kernels, tail_pass(): pl.pallas_call(functools.partial(tail_kernel, group), out_shape=(shape((r...  147 us
    pallas_call x1, Pallas kernels, layer_pass(): pl.pallas_call(functools.partial(layer_kernel, group), out_shape=(whole,...  136 us
    convert_element_type x1, other arithmetic, body(): up_grad.astype(f32)  6.81 us

commit v1 on v0

--- a/solution.py
+++ b/solution.py
@@ -3,6 +3,7 @@
 
 import jax
 import jax.numpy as jnp
+import numpy as np
 from jax import lax
 from jax.experimental import pallas as pl
 from jax.experimental.pallas import tpu as pltpu
@@ -62,6 +63,14 @@
     pl.semaphore_wait(pltpu.get_barrier_semaphore(), count)
 
 
+def pair_of(ctx, group):
+    if group != 8:
+        return ctx
+    return ctx + jnp.where(
+        (ctx == 1) | (ctx == 4), 2, jnp.where((ctx == 3) | (ctx == 6), -2, 0)
+    )
+
+
 def pair_order(z, depth):
     return [
         z,
@@ -73,14 +82,16 @@
 
 def layer_kernel(group, *refs):
     hidden, grad, w_up_in, w_down_in, w_qkv_in, w_out = refs[:6]
-    norms, bias_up, bias_qkv, inverse, seg_len, seg_parent = refs[6:12]
-    h_out, g_out, x_out, heads_out, part_out, back_out, pairs_out, cols_out = refs[12:20]
-    tables, sums, bias_sum = refs[20:23]
-    h_buf, g_buf, w_up, w_down, w_qkv, x_mlp, x_attn, act, slope, pre_grad = refs[23:33]
-    heads, part, back, down_grad, up_grad, core_buf, mean, rstd = refs[33:41]
-    own_sem, y_send, y_recv, up_send, up_recv, down_send, down_recv = refs[41:48]
-    weight_sem, pair_sem, grad_sem, head_send, head_recv = refs[48:53]
-    core_send, core_recv, cols_send, cols_recv = refs[53:57]
+    vectors, (inverse, seg_len, seg_parent), refs = refs[6:14], refs[14:17], refs[7:]
+    h_out, g_out, x_out, heads_out, part_out, back_out, pairs_out, early_out, cols_out = refs[10:19]
+    tables, sums, bias_sum, local_sum, norms = refs[19:24]
+    h_buf, g_buf, w_up, w_down, w_qkv, x_mlp, x_attn, act, slope, pre_grad = refs[24:34]
+    heads, part, back, down_grad, up_grad, core_buf, mean, rstd, bias_up, bias_qkv = refs[34:44]
+    all_qkv, all_up = refs[44:46]
+    refs = refs[2:]
+    own_sem, y_send, y_recv, up_send, up_recv, down_send, down_recv = refs[44:51]
+    weight_sem, pair_sem, grad_sem, head_send, head_recv = refs[51:56]
+    core_send, core_recv, cols_send, cols_recv, early_send, early_recv = refs[56:62]
     dp, ctx, z, y, depth = place(group)
     bufs, sources, outs = (h_buf, g_buf), (hidden, grad), (h_out, g_out)
     rows = hidden.shape[0]
@@ -134,32 +145,30 @@
             below,
         )
 
-    def relay(i, k):
-        @pl.when(z >= k)
-        def _():
-            at_z = jnp.maximum(z - k, 0)
-            upward(i, at_z).wait_recv()
-            pl.when(has_above)(lambda: upward(i, at_z).start())
-
-        @pl.when(z + k < depth)
-        def _():
-            at_z = jnp.minimum(z + k, depth - 1)
-            downward(i, at_z).wait_recv()
-            pl.when(has_below)(lambda: downward(i, at_z).start())
+    def relay_up(i, k):
+        at_z = jnp.maximum(z - k, 0)
+        upward(i, at_z).wait_recv()
+        pl.when(has_above)(lambda: upward(i, at_z).start())
+
+    def relay_down(i, k):
+        at_z = jnp.minimum(z + k, depth - 1)
+        downward(i, at_z).wait_recv()
+        pl.when(has_below)(lambda: downward(i, at_z).start())
 
     def turn(n):
         if n < depth:
-            relay(0, n)
+            pl.when(z >= n)(lambda: relay_up(0, n))
+            pl.when(z + n < depth)(lambda: relay_down(0, n))
+            to_other(0, order[n]).start()
             pl.when((z == n - 1) & has_above)(lambda: upward(1, z, sources[1]).start())
             pl.when((z == depth - n) & has_below)(lambda: downward(1, z, sources[1]).start())
-            to_other(0, order[n]).start()
-        else:
-            if n < 2 * depth - 1:
-                relay(1, n - depth + 1)
-            if n == depth:
-                to_other(1, z, sources[1]).start()
-            else:
-                to_other(1, order[n - depth]).start()
+        for k in range(1, depth):
+            pl.when((z == n - k) & (z >= k))(lambda k=k: relay_up(1, k))
+            pl.when((depth - 1 - z == n - k) & (z + k < depth))(lambda k=k: relay_down(1, k))
+        if n == depth:
+            to_other(1, z, sources[1]).start()
+        if n > depth:
+            to_other(1, order[n - depth]).start()
 
     def y_arrive(i, s):
         here = chunk(i, order[s], 1 - y)
@@ -220,6 +229,17 @@
 
     sums[...] = jnp.zeros_like(sums)
     bias_sum[...] = jnp.zeros_like(bias_sum)
+    for n in range(6):
+        norms[n : n + 1, :] = vectors[n][...].astype(f32).reshape(1, columns)
+    norms[6:8, :] = jnp.zeros((2, columns), f32)
+
+    def take_mine(target, vector, wide_row):
+        wide_row[...] = vector[...].astype(f32).reshape(wide_row.shape)
+        size = target.shape[1]
+        target[...] = wide_row[:, pl.ds(pl.multiple_of(ctx * size, HEAD_DIM), size)]
+
+    take_mine(bias_qkv, vectors[6], all_qkv)
+    take_mine(bias_up, vectors[7], all_up)
 
     def normalize(s):
         step = 32
@@ -339,19 +359,30 @@
             grad_half(t, core), pairs_out.at[pl.ds(t * half, half)], grad_sem.at[t]
         )
 
-    def outer(n, left, right):
-        for m in range(tiles):
+    def outer(n, left, right, last, ms=range(units // tall)):
+        first, second = (pair_at(2), pair_at(3)) if last else (pair_at(0), pair_at(1))
+        for m in ms:
             mine = pl.ds(m * tall, tall)
 
             @pl.loop(0, columns // (2 * wide))
             def _(k):
                 cols = pl.ds(pl.multiple_of(k * 2 * wide, 2 * wide), 2 * wide)
-                held[n][mine, cols] = dot_tn(left[:, mine], right[:, cols]).astype(bf16)
-
-            to_core(n * tiles + m).start()
-
-    def outer_sum(n):
-        for t in range(n * tiles, (n + 1) * tiles):
+                term = dot_tn(left[first, mine], right[first, cols])
+                term += dot_tn(left[second, mine], right[second, cols])
+                if last:
+                    term += held[n][mine, cols].astype(f32)
+                held[n][mine, cols] = term.astype(bf16)
+
+            if last:
+                to_core(n * tiles + m).start()
+
+    def early_x(t):
+        return copy_to(
+            grad_half(t, core), early_out.at[t], early_send.at[t], early_recv.at[t], across
+        )
+
+    def outer_sum(ts):
+        for t in ts:
             to_core(t).wait_recv()
             mine = grad_half(t, core)
 
@@ -363,6 +394,8 @@
                 )
 
             grad_keep(t).start()
+            if t < early_out.shape[0]:
+                early_x(t).start()
 
     share = cols_out.shape[2]
 
@@ -370,7 +403,7 @@
         owner = lax.rem(ctx + n, group)
         block = w_out.at[
             pl.ds(pl.multiple_of(dp * share, share), share),
-            pl.ds(pl.multiple_of(owner * head_cols, head_cols), head_cols),
+            pl.ds(pl.multiple_of(pair_of(owner, group) * head_cols, head_cols), head_cols),
         ]
         if n == 0:
             return pltpu.make_async_copy(block, cols_out.at[ctx, dp], cols_send.at[0])
@@ -394,15 +427,28 @@
         return copy_to(here, here, cols_send.at[group + 1], cols_recv.at[group + 1], across)
 
     def to_head(j):
-        target = lax.rem(3 * ctx + j, group)
+        block = 3 * ctx + j
+        kind, target = lax.div(block, group), pair_of(lax.rem(block, group), group)
         remote = copy_to(
-            heads.at[j], heads_out.at[j], head_send.at[j], head_recv.at[j], (dp, target)
-        )
-        local = pltpu.make_async_copy(heads.at[j], heads_out.at[j], head_recv.at[j])
+            heads.at[j], heads_out.at[kind], head_send.at[j], head_recv.at[kind], (dp, target)
+        )
+        local = pltpu.make_async_copy(heads.at[j], heads_out.at[kind], head_send.at[j])
         return target == ctx, remote, local
 
-    for n in range(group):
-        to_columns(n).start()
+    def send_heads(crossing):
+        for j in range(3):
+            here, remote, local = to_head(j)
+            target = pair_of(lax.rem(3 * ctx + j, group), group)
+            crosses = target % RAILS != ctx % RAILS
+            if crossing:
+                pl.when(crosses)(lambda remote=remote: remote.start())
+            else:
+                pl.when(here)(lambda local=local: local.start())
+                pl.when(jnp.logical_not(here | crosses))(lambda remote=remote: remote.start())
+
+    def head_source(kind):
+        return lax.div(kind * group + pair_of(ctx, group), 3)
+
     turn(1)
     own[0].wait()
     y_arrive(0, 0)
@@ -414,32 +460,38 @@
     y_arrive(0, 2)
     forward(2)
     turn(4)
+    for n in range(group):
+        to_columns(n).start()
     y_arrive(0, 3)
     forward(3)
     turn(5)
+    send_heads(False)
     own[1].wait()
     y_arrive(1, 0)
     backward(0)
+    at = pl.ds(pl.multiple_of(ctx * rows, rows), rows)
+    local_sum[...] = jnp.sum(g_buf[at, :].astype(f32), axis=0, keepdims=True)
     turn(6)
     y_arrive(1, 1)
     backward(1)
     turn(7)
-    for j in range(3):
-        here, remote, local = to_head(j)
-        pl.when(here)(lambda local=local: local.start())
-        pl.when(jnp.logical_not(here))(lambda remote=remote: remote.start())
     columns_arrive()
     columns_core(core).start()
+    outer(0, act, g_buf, False)
+    outer(1, pre_grad, x_mlp, False)
+    columns_core(1 - core).wait_recv()
+    columns_x(x).start()
     y_arrive(1, 2)
     backward(2)
-    columns_core(1 - core).wait_recv()
-    columns_x(x).start()
+    send_heads(True)
     y_arrive(1, 3)
     backward(3)
-    outer(0, act, g_buf)
-    outer(1, pre_grad, x_mlp)
-    outer_sum(0)
-    outer_sum(1)
+    early = early_out.shape[0]
+    outer(0, act, g_buf, True, range(early + 1))
+    outer_sum(range(early))
+    outer(0, act, g_buf, True, range(early + 1, tiles))
+    outer(1, pre_grad, x_mlp, True)
+    outer_sum(range(early, 2 * tiles))
 
     for at_z in range(depth):
         to_other(0, at_z).wait_send()
@@ -451,8 +503,11 @@
         here, remote, local = to_head(j)
         pl.when(here)(lambda local=local: local.wait())
         pl.when(jnp.logical_not(here))(lambda remote=remote: remote.wait_send())
-        source = lax.rem(pow(3, -1, group) * (ctx + group - j), group)
-        pl.when(source != ctx)(lambda remote=remote: remote.wait_recv())
+    for kind in range(3):
+        arriving = copy_to(
+            heads.at[0], heads_out.at[kind], head_send.at[0], head_recv.at[kind], other
+        )
+        pl.when(head_source(kind) != ctx)(lambda arriving=arriving: arriving.wait_recv())
     for s in range(4):
         keep(0, s, h_buf, h_out).wait()
         keep(1, s, x_attn, x_out).wait()
@@ -464,19 +519,23 @@
         grad_keep(t).wait()
     for n in range(1, group):
         to_columns(n).wait_send()
+    for t in range(early):
+        early_x(t).wait_send()
+        early_x(t).wait_recv()
     columns_core(core).wait_send()
     columns_x(x).wait_send()
     columns_x(1 - x).wait_recv()
 
 
 def layer_pass(
-    group, hidden, grad, w_up, w_down, w_qkv, w_out, norms, bias_up, bias_qkv, seg_len, seg_parent
+    group, hidden, grad, w_up, w_down, w_qkv, w_out, vectors, seg_len, seg_parent
 ):
     rows, columns = hidden.shape
     tokens, units, head_cols = group * rows, w_up.shape[0], w_qkv.shape[0] // 3
     depth = group // RAILS
-    inverse = jnp.power(10000.0, -2.0 * jnp.arange(ROT_DIM // 2, dtype=f32) / ROT_DIM)
-    inverse = jnp.broadcast_to(inverse[:, None], (ROT_DIM // 2, rows))
+    inverse = 10000.0 ** (-2.0 * np.arange(ROT_DIM // 2) / ROT_DIM)
+    inverse = jnp.asarray(np.broadcast_to(inverse[:, None], (ROT_DIM // 2, rows)), f32)
+    early = 1
     sems = pltpu.SemaphoreType.DMA
     shape = jax.ShapeDtypeStruct
     anywhere = pl.BlockSpec(memory_space=pl.ANY)
@@ -495,13 +554,16 @@
             whole,
             whole,
             shape((units, columns), bf16),
+            shape((early, half, columns), bf16),
             shape((group, copies, columns // group // copies, head_cols), bf16),
             shape((4, tokens, HEAD_DIM), f32),
             shape((2, columns), f32),
             shape((1, units), f32),
+            shape((1, columns), f32),
+            shape((8, columns), f32),
         ),
-        in_specs=[anywhere] * 6 + [vmem] * 4 + [smem] * 2,
-        out_specs=[anywhere] * 8 + [vmem] * 3,
+        in_specs=[anywhere] * 6 + [vmem] * 9 + [smem] * 2,
+        out_specs=[anywhere] * 9 + [vmem] * 5,
         scratch_shapes=[pltpu.VMEM((tokens, columns), bf16)] * 2
         + [pltpu.VMEM((units, columns), bf16)] * 2
         + [pltpu.VMEM((3 * head_cols, columns), bf16)]
@@ -512,23 +574,26 @@
         + [pltpu.VMEM((units, columns), bf16)] * 2
         + [pltpu.VMEM((units // half, half, columns), bf16)]
         + [pltpu.VMEM((tokens, 1), f32)] * 2
+        + [pltpu.VMEM((1, units), f32), pltpu.VMEM((1, 3 * head_cols), f32)]
+        + [pltpu.VMEM((1, vector.shape[0]), f32) for vector in vectors[6:]]
         + [sems((2,))]
         + [sems((2, depth))] * 6
         + [sems((3,)), sems((5, 4)), sems((units // half,)), sems((3,)), sems((3,))]
         + [sems((units // half,))] * 2
-        + [sems((group + 2,))] * 2,
+        + [sems((group + 2,))] * 2
+        + [sems((early,))] * 2,
         compiler_params=pltpu.CompilerParams(
-            collective_id=0, has_side_effects=True, vmem_limit_bytes=61 * 2**20
+            collective_id=0, has_side_effects=True, vmem_limit_bytes=62 * 2**20
         ),
         name="layer_pass",
-    )(hidden, grad, w_up, w_down, w_qkv, w_out, norms, bias_up, bias_qkv, inverse, seg_len, seg_parent)
+    )(hidden, grad, w_up, w_down, w_qkv, w_out, *vectors, inverse, seg_len, seg_parent)
 
 
 def tail_kernel(group, *refs):
     pairs, arrived_in, grad_in, w_cols_in, part_in, back_in, x_in, w_qkv_in, hidden_in = refs[:9]
-    tables_in, norms, mlp_sums, up_sums, local_sums, seg_len, seg_parent = refs[9:16]
-    part_out, back_out, down_out, up_out, out_out, qkv_out, vectors_out = refs[16:23]
-    refs = refs[23:]
+    tables_in, early_in, norms, mlp_sums, up_sums, local_sums, seg_len, seg_parent = refs[9:17]
+    part_out, back_out, down_out, up_out, out_out, qkv_out, vectors_out, stats_out = refs[17:25]
+    refs = refs[25:]
     arrived, g_buf, w_cols, part, back, x_buf, w_qkv, h_buf, tables = refs[:9]
     att_grad, attended, returns, returned, y_buf, z_buf = refs[9:15]
     out_grad, qkv_grad, qkv_core, out_core, out_rows, from_x, pairs_x, key_acc, value_acc = refs[15:24]
@@ -601,11 +666,12 @@
             across,
         )
 
-    for t in range(pair_tiles):
+    early = early_in.shape[0]
+    for t in range(early, pair_tiles):
         pair_x(t).start()
     loads = [
-        pltpu.make_async_copy(source, held, load_sem.at[n])
-        for n, (source, held) in enumerate(
+        pltpu.make_async_copy(source, target, load_sem.at[n])
+        for n, (source, target) in enumerate(
             (
                 (w_cols_in, w_cols),
                 (grad_in, g_buf),
@@ -616,6 +682,7 @@
                 (back_in, back),
                 (hidden_in, h_buf),
                 (x_in, x_buf),
+                (early_in, pairs_x.at[pl.ds(0, early)]),
             )
         )
     ]
@@ -645,7 +712,6 @@
         at = at + seg_len[0, n]
     loads[2].wait()
     loads[3].wait()
-    slots = [lax.rem(kind * group + ctx, 3) for kind in range(3)]
 
     def unturn(values, at):
         return (
@@ -670,9 +736,9 @@
                 reach = jnp.where(token >= starts[k], reaches[k], reach)
                 label = jnp.where(key >= starts[k], 1 << k, label)
             allowed = ((reach & label) != 0) & (key <= token)
-            query = arrived[slots[0], mine, lanes]
-            keys = arrived[slots[1], upto, lanes]
-            values = arrived[slots[2], upto, lanes]
+            query = arrived[0, mine, lanes]
+            keys = arrived[1, upto, lanes]
+            values = arrived[2, upto, lanes]
             out_grad_rows = att_grad[mine, lanes]
             scores = jnp.where(allowed, dot_nt(query, keys) * scale, masked_score)
             expo = jnp.exp(scores - jnp.max(scores, axis=1, keepdims=True))
@@ -683,27 +749,26 @@
             delta = jnp.sum(probs * prob_grad, axis=1, keepdims=True)
             score_grad = (probs * (prob_grad - delta)).astype(bf16)
             query_grad = dot_nn(score_grad, keys) * scale
-            returns[slots[0], mine, lanes] = unturn(query_grad, mine).astype(bf16)
+            returns[0, mine, lanes] = unturn(query_grad, mine).astype(bf16)
             key_acc[upto, :] += dot_tn(score_grad, query)
             value_acc[upto, :] += dot_tn(weights, out_grad_rows)
 
         for n in range(tokens // tall):
             mine = pl.ds(n * tall, tall)
-            returns[slots[1], mine, lanes] = unturn(key_acc[mine, :] * scale, mine).astype(bf16)
-            returns[slots[2], mine, lanes] = value_acc[mine, :].astype(bf16)
-
-    back_step = pow(3, -1, group)
-
-    def to_owner(j):
-        owner = lax.rem(back_step * (ctx + group - j), group)
+            returns[1, mine, lanes] = unturn(key_acc[mine, :] * scale, mine).astype(bf16)
+            returns[2, mine, lanes] = value_acc[mine, :].astype(bf16)
+
+    def to_owner(kind):
+        block = kind * group + pair_of(ctx, group)
+        owner, slot = lax.div(block, 3), lax.rem(block, 3)
         remote = copy_to(
-            returns.at[j], returned.at[j], head_send.at[j], head_recv.at[j], (dp, owner)
-        )
-        local = pltpu.make_async_copy(returns.at[j], returned.at[j], head_recv.at[j])
+            returns.at[kind], returned.at[slot], head_send.at[kind], head_recv.at[slot], (dp, owner)
+        )
+        local = pltpu.make_async_copy(returns.at[kind], returned.at[slot], head_send.at[kind])
         return owner == ctx, remote, local
 
-    for j in range(3):
-        here, remote, local = to_owner(j)
+    for kind in range(3):
+        here, remote, local = to_owner(kind)
         pl.when(here)(lambda local=local: local.start())
         pl.when(jnp.logical_not(here))(lambda remote=remote: remote.start())
 
@@ -735,6 +800,68 @@
                 part[at, cols].astype(f32) + dot_nt(attended[at, :], w_cols[cols, :])
             ).astype(bf16)
 
+    low = z < depth // 2
+    order = [
+        jnp.where(low, depth - 1, 0),
+        jnp.where(low, depth - 2, 1),
+        jnp.where(low, 1 - z, 2 * depth - 3 - z),
+        z,
+    ]
+    parts = (part, back)
+
+    def chunk(i, at_z, at_y):
+        return parts[i].at[pl.ds(pl.multiple_of((at_z * RAILS + at_y) * rows, rows), rows)]
+
+    def swap(i, s):
+        return copy_to(
+            chunk(i, order[s], 1 - y),
+            y_buf.at[i, order[s]],
+            y_send.at[i, s],
+            y_recv.at[i, s],
+            other,
+        )
+
+    def upward(i, at):
+        return copy_to(
+            chunk(i, at, y), z_buf.at[i, at], up_send.at[i, at], up_recv.at[i, at], above
+        )
+
+    def downward(i, at, slot):
+        return copy_to(
+            chunk(i, at, y), z_buf.at[i, slot], down_send.at[i, at], down_recv.at[i, at], below
+        )
+
+    def down_slot(at, owner_z):
+        return jnp.where(at == owner_z, depth, at)
+
+    def scatter_step(i, s):
+        at = order[s]
+        swap(i, s).wait_recv()
+        mine = chunk(i, at, y)
+        add(mine, mine, y_buf.at[i, at])
+
+        @pl.when((at >= z) & has_below)
+        def _():
+            upward(i, at).wait_recv()
+            add(mine, mine, z_buf.at[i, at])
+
+        @pl.when((at <= z) & has_above)
+        def _():
+            slot = down_slot(at, z)
+            downward(i, at, slot).wait_recv()
+            add(mine, mine, z_buf.at[i, slot])
+
+        pl.when(at > z)(lambda: upward(i, at).start())
+        pl.when(at < z)(lambda: downward(i, at, down_slot(at, z - 1)).start())
+
+    results = (part_out, back_out)
+
+    def scatter_out(i):
+        return pltpu.make_async_copy(chunk(i, z, y), results[i], result_sem.at[i])
+
+    for s in range(depth):
+        swap(0, s).start()
+
     out_to_core.wait_recv()
 
     @pl.loop(0, group)
@@ -744,7 +871,7 @@
             + out_grad[n, pl.ds(pl.multiple_of(core * half, half), half), :].astype(f32)
         ).astype(bf16)
 
-    my_cols = pl.ds(pl.multiple_of(ctx * head_cols, head_cols), head_cols)
+    my_cols = pl.ds(pl.multiple_of(pair_of(ctx, group) * head_cols, head_cols), head_cols)
 
     def out_block(n):
         owner = lax.rem(ctx + n, group)
@@ -761,73 +888,65 @@
     own_block = pltpu.make_async_copy(out_core.at[ctx], out_rows.at[:, my_cols], block_send.at[0])
     own_block.start()
 
-    low = z < depth // 2
-    order = [
-        jnp.where(low, depth - 1, 0),
-        jnp.where(low, depth - 2, 1),
-        jnp.where(low, 1 - z, 2 * depth - 3 - z),
-        z,
-    ]
-    parts = (part, back)
-
-    def chunk(i, at_z, at_y):
-        return parts[i].at[pl.ds(pl.multiple_of((at_z * RAILS + at_y) * rows, rows), rows)]
-
-    def swap(i, s):
+    again = pltpu.make_async_copy(pairs, g_buf, sum_sem.at[0])
+    again.start()
+
+    def qkv_half(t, which):
+        start = pl.multiple_of(t * 2 * half + which * half, half)
+        return qkv_grad.at[pl.ds(start, half)]
+
+    def to_core(t):
         return copy_to(
-            chunk(i, order[s], 1 - y),
-            y_buf.at[i, order[s]],
-            y_send.at[i, s],
-            y_recv.at[i, s],
-            other,
-        )
-
-    def upward(i, at):
-        return copy_to(
-            chunk(i, at, y), z_buf.at[i, at], up_send.at[i, at], up_recv.at[i, at], above
-        )
-
-    def downward(i, at, slot):
-        return copy_to(
-            chunk(i, at, y), z_buf.at[i, slot], down_send.at[i, at], down_recv.at[i, at], below
-        )
-
-    def down_slot(at, owner_z):
-        return jnp.where(at == owner_z, depth, at)
-
-    def scatter_step(i, s):
-        at = order[s]
-        swap(i, s).wait_recv()
-        mine = chunk(i, at, y)
-        add(mine, mine, y_buf.at[i, at])
-
-        @pl.when((at >= z) & has_below)
-        def _():
-            upward(i, at).wait_recv()
-            add(mine, mine, z_buf.at[i, at])
-
-        @pl.when((at <= z) & has_above)
-        def _():
-            slot = down_slot(at, z)
-            downward(i, at, slot).wait_recv()
-            add(mine, mine, z_buf.at[i, slot])
-
-        pl.when(at > z)(lambda: upward(i, at).start())
-        pl.when(at < z)(lambda: downward(i, at, down_slot(at, z - 1)).start())
-
-    results = (part_out, back_out)
-
-    def scatter_out(i):
-        return pltpu.make_async_copy(chunk(i, z, y), results[i], result_sem.at[i])
-
-    for s in range(depth):
-        swap(0, s).start()
-
+            qkv_half(t, 1 - core), qkv_core.at[t], core_send.at[t], core_recv.at[t], sibling
+        )
+
+    def across_x(t):
+        source = qkv_half(t, core) if t < core_tiles else out_rows
+        return copy_to(source, from_x.at[t], x_send.at[t], x_recv.at[t], across)
+
+    spots = (
+        [(down_out, 2 * half * t) for t in range(pair_tiles // 2)]
+        + [(up_out, 2 * half * t) for t in range(pair_tiles // 2)]
+        + [(qkv_out, 2 * half * t) for t in range(core_tiles)]
+        + [(out_out, 0)]
+    )
+    def total_of(t):
+        return pairs_x.at[t] if t < pair_tiles else from_x.at[t - pair_tiles]
+
+    def spot(t, which):
+        array, first = spots[t]
+        return array.at[pl.ds(pl.multiple_of(first + which * half, half), half)]
+
+    def keep(t):
+        return pltpu.make_async_copy(total_of(t), spot(t, core), keep_sem.at[t])
+
+    def finish(t, which):
+        return copy_to(total_of(t), spot(t, which), done_send.at[t], done_recv.at[t], sibling)
+
+    def x_sum(t):
+        total = total_of(t)
+        if t < pair_tiles:
+            if t >= early:
+                pair_x(t).wait_recv()
+            add(total, total, g_buf.at[pl.ds(t * half, half)])
+        else:
+            n = t - pair_tiles
+            across_x(n).wait_recv()
+            add(total, total, qkv_half(n, core) if n < core_tiles else out_rows)
+        keep(t).start()
+        finish(t, core).start()
+
+    loads[9].wait()
+    again.wait()
+    x_sum(0)
     for j in range(3):
         here, remote, local = to_owner(j)
         pl.when(here)(lambda local=local: local.wait())
-        target = lax.rem(3 * ctx + j, group)
-        pl.when(target != ctx)(lambda remote=remote: remote.wait_recv())
+        source = pair_of(lax.rem(3 * ctx + j, group), group)
+        arriving = copy_to(
+            returns.at[0], returned.at[j], head_send.at[0], head_recv.at[j], other
+        )
+        pl.when(source != ctx)(lambda arriving=arriving: arriving.wait_recv())
     for n in (5, 6, 7):
         loads[n].wait()
     sums[...] = jnp.zeros_like(sums)
@@ -894,16 +1013,6 @@
         swap(1, s).start()
 
     loads[8].wait()
-
-    def qkv_half(t, which):
-        start = pl.multiple_of(t * 2 * half + which * half, half)
-        return qkv_grad.at[pl.ds(start, half)]
-
-    def to_core(t):
-        return copy_to(
-            qkv_half(t, 1 - core), qkv_core.at[t], core_send.at[t], core_recv.at[t], sibling
-        )
-
     for t in range(core_tiles):
 
         @pl.loop(0, columns // (2 * wide))
@@ -915,72 +1024,43 @@
 
         to_core(t).start()
 
-    def across_x(t):
-        source = qkv_half(t, core) if t < core_tiles else out_rows
-        return copy_to(source, from_x.at[t], x_send.at[t], x_recv.at[t], across)
-
-    spots = (
-        [(down_out, 2 * half * t) for t in range(pair_tiles // 2)]
-        + [(up_out, 2 * half * t) for t in range(pair_tiles // 2)]
-        + [(qkv_out, 2 * half * t) for t in range(core_tiles)]
-        + [(out_out, 0)]
-    )
-    again = pltpu.make_async_copy(pairs, g_buf, sum_sem.at[0])
-    again.start()
-
-    def total_of(t):
-        return pairs_x.at[t] if t < pair_tiles else from_x.at[t - pair_tiles]
-
-    def spot(t, which):
-        array, first = spots[t]
-        return array.at[pl.ds(pl.multiple_of(first + which * half, half), half)]
-
-    def keep(t):
-        return pltpu.make_async_copy(total_of(t), spot(t, core), keep_sem.at[t])
-
-    def finish(t, which):
-        return copy_to(total_of(t), spot(t, which), done_send.at[t], done_recv.at[t], sibling)
-
-    def x_sum(t):
-        total = total_of(t)
-        if t < pair_tiles:
-            pair_x(t).wait_recv()
-            add(total, total, g_buf.at[pl.ds(t * half, half)])
-        else:
-            n = t - pair_tiles
-            across_x(n).wait_recv()
-            add(total, total, qkv_half(n, core) if n < core_tiles else out_rows)
-        keep(t).start()
-        finish(t, core).start()
-
     for t in range(core_tiles):
         to_core(t).wait_recv()
         mine = qkv_half(t, core)
         add(mine, mine, qkv_core.at[t])
         across_x(t).start()
+    stats_out[...] = tables[3, pl.ds(pl.multiple_of(ctx * rows, rows), rows), :]
+    for s in range(depth):
+        scatter_step(0, s)
+        if s == 0:
+            x_sum(1)
+            x_sum(2)
+        x_sum(3 + s)
+    scatter_out(0).start()
     own_block.wait()
     for n in range(1, group):
         source = lax.rem(ctx + group - n, group)
-        theirs = pl.ds(pl.multiple_of(source * head_cols, head_cols), head_cols)
+        theirs = pl.ds(
+            pl.multiple_of(pair_of(source, group) * head_cols, head_cols), head_cols
+        )
         copy_to(
             out_core.at[ctx], out_rows.at[:, theirs], block_send.at[n], block_recv.at[n], other
         ).wait_recv()
-    again.wait()
-    for s in range(depth):
-        scatter_step(0, s)
-        x_sum(2 * s)
-        x_sum(2 * s + 1)
-    scatter_out(0).start()
+    across_x(core_tiles).start()
     vector_step(1)
-    for s in range(depth):
-        scatter_step(1, s)
-        if s < 2:
-            vector_step(s + 2)
-        if s == 1:
-            across_x(core_tiles).start()
-        x_sum(pair_tiles + s)
+    x_sum(7)
+    scatter_step(1, 0)
+    vector_step(2)
+    x_sum(pair_tiles)
+    scatter_step(1, 1)
+    vector_step(3)
+    x_sum(pair_tiles + 1)
+    scatter_step(1, 2)
+    x_sum(pair_tiles + 2)
+    scatter_step(1, 3)
+    scatter_out(1).start()
+    x_sum(pair_tiles + 3)
     vector_step(4)
-    scatter_out(1).start()
 
     for j in range(3):
         here, remote, local = to_owner(j)
@@ -992,7 +1072,7 @@
         to_core(t).wait_send()
     for t in range(core_tiles + 1):
         across_x(t).wait_send()
-    for t in range(pair_tiles):
+    for t in range(early, pair_tiles):
         pair_x(t).wait_send()
     for t in range(len(spots)):
         keep(t).wait()
@@ -1023,6 +1103,7 @@
     w_qkv,
     hidden_all,
     tables,
+    early,
     norms,
     mlp_sums,
     up_sums,
@@ -1058,9 +1139,10 @@
             shape((2 * half, columns), bf16),
             shape(w_qkv.shape, bf16),
             shape((vectors, lane_cols), f32),
+            shape((rows, HEAD_DIM), f32),
         ),
-        in_specs=[anywhere] * 10 + [small] * 4 + [smem] * 2,
-        out_specs=[anywhere] * 6 + [small],
+        in_specs=[anywhere] * 11 + [small] * 4 + [smem] * 2,
+        out_specs=[anywhere] * 6 + [small] * 2,
         scratch_shapes=[
             vmem(arrived.shape, bf16),
             whole,
@@ -1088,7 +1170,7 @@
             vmem((tokens, HEAD_DIM), f32),
             vmem((2, columns), f32),
             vmem((10, vectors, lane_cols), f32),
-            sems((9,)),
+            sems((10,)),
         ]
         + [sems((2, depth))] * 6
         + [sems((2,)), sems((3,)), sems((3,)), sems((pair_tiles,)), sems((pair_tiles,))]
@@ -1099,7 +1181,7 @@
         + [sems((5,))] * 2
         + [sems((1,))],
         compiler_params=pltpu.CompilerParams(
-            collective_id=1, has_side_effects=True, vmem_limit_bytes=61 * 2**20
+            collective_id=1, has_side_effects=True, vmem_limit_bytes=62 * 2**20
         ),
         name="tail_pass",
     )(
@@ -1113,6 +1195,7 @@
         w_qkv,
         hidden_all,
         tables,
+        early,
         norms,
         mlp_sums,
         up_sums,
@@ -1120,6 +1203,89 @@
         seg_len,
         seg_parent,
     )
+
+
+def finish_kernel(*refs):
+    grads, (hidden, grad, summed, w_sum, stats, norms, vectors) = refs[:4], refs[4:11]
+    outs, (hidden_out, grad_in), vector_outs = refs[11:15], refs[15:17], refs[17:25]
+    narrow, wide, in_sem, out_sem = refs[25:]
+    tall = narrow.shape[1]
+    tiles = [(n, m) for n in range(4) for m in range(grads[n].shape[0] // tall)]
+
+    def fetch(t):
+        n, m = tiles[t]
+        return pltpu.make_async_copy(
+            grads[n].at[pl.ds(m * tall, tall)], narrow.at[t], in_sem.at[t]
+        )
+
+    def store(t):
+        n, m = tiles[t]
+        return pltpu.make_async_copy(wide.at[t], outs[n].at[pl.ds(m * tall, tall)], out_sem.at[t])
+
+    for t in range(len(tiles)):
+        fetch(t).start()
+    rows = 32
+    for t in range(len(tiles)):
+        fetch(t).wait()
+
+        @pl.loop(0, tall // rows)
+        def _(n):
+            at = pl.ds(pl.multiple_of(n * rows, rows), rows)
+            wide[t, at, :] = narrow[t, at, :].astype(f32)
+
+        store(t).start()
+
+    @pl.loop(0, hidden.shape[0] // rows)
+    def _(n):
+        at = pl.ds(pl.multiple_of(n * rows, rows), rows)
+        values = hidden[at, :].astype(f32)
+        hidden_out[at, :] = (
+            values + summed[at, :].astype(f32) + norms[4:5, :] + norms[5:6, :]
+        ).astype(bf16)
+        rstd = stats[at, 1:2]
+        normed = (values - stats[at, 0:1]) * rstd
+        back = w_sum[at, :].astype(f32)
+        along = jnp.mean(back * normed, axis=1, keepdims=True)
+        grad_in[at, :] = (
+            grad[at, :].astype(f32)
+            + (back - jnp.mean(back, axis=1, keepdims=True) - normed * along) * rstd
+        )
+
+    lane_cols = vectors.shape[1]
+    places = [0, 1, 2, 3, 4, 4, 5, 8]
+    each = hidden.shape[1] // lane_cols
+    for out, place_of in zip(vector_outs, places):
+        for n in range(out.shape[0] // lane_cols):
+            out[pl.ds(n * lane_cols, lane_cols)] = vectors[place_of * each + n, :]
+    for t in range(len(tiles)):
+        store(t).wait()
+
+
+def finish_pass(down, up, qkv, out, hidden, grad, summed, w_sum, stats, norms, vectors):
+    tall = 256
+    columns = hidden.shape[1]
+    grads = (down, up, qkv, out)
+    tiles = sum(array.shape[0] for array in grads) // tall
+    shape = jax.ShapeDtypeStruct
+    anywhere = pl.BlockSpec(memory_space=pl.ANY)
+    vmem = pl.BlockSpec(memory_space=pltpu.VMEM)
+    lengths = [columns] * 6 + [3 * columns, vectors.size - 8 * columns]
+    return pl.pallas_call(
+        finish_kernel,
+        out_shape=[shape(array.shape, f32) for array in grads]
+        + [shape(hidden.shape, bf16), shape(hidden.shape, f32)]
+        + [shape((length,), f32) for length in lengths],
+        in_specs=[anywhere] * 4 + [vmem] * 7,
+        out_specs=[anywhere] * 4 + [vmem] * 10,
+        scratch_shapes=[
+            pltpu.VMEM((tiles, tall, columns), bf16),
+            pltpu.VMEM((tiles, tall, columns), f32),
+            pltpu.SemaphoreType.DMA((tiles,)),
+            pltpu.SemaphoreType.DMA((tiles,)),
+        ],
+        compiler_params=pltpu.CompilerParams(vmem_limit_bytes=56 * 2**20),
+        name="finish_pass",
+    )(*grads, hidden, grad, summed, w_sum, stats, norms, vectors)
 
 
 def body(
@@ -1141,14 +1307,17 @@
     bias_down,
 ):
     group = lax.axis_size("ctx")
-    me = lax.axis_index("ctx")
-    local_rows = hidden_in.shape[1]
-    tokens = local_rows * group
-    head_count = HEADS // group
-    head_cols = head_count * HEAD_DIM
-    norms = jnp.stack([gain_attn, shift_attn, gain_mlp, shift_mlp]).astype(f32)
-    up_bias = lax.dynamic_slice_in_dim(bias_up, me * w_up.shape[0], w_up.shape[0])
-    qkv_bias = lax.dynamic_slice_in_dim(bias_qkv, me * 3 * head_cols, 3 * head_cols)
+    head_cols = HEADS // group * HEAD_DIM
+    vectors = (
+        gain_attn,
+        shift_attn,
+        gain_mlp,
+        shift_mlp,
+        bias_out,
+        bias_down,
+        bias_qkv,
+        bias_up,
+    )
     (
         hidden_all,
         grad_all,
@@ -1157,10 +1326,13 @@
         mlp_part,
         mlp_back,
         pairs,
+        early,
         w_cols,
         tables,
         mlp_sums,
         up_sums,
+        local_sums,
+        norms,
     ) = layer_pass(
         group,
         hidden_in[0],
@@ -1169,14 +1341,11 @@
         w_down,
         w_qkv,
         w_out,
-        norms,
-        up_bias.astype(f32)[None],
-        qkv_bias.astype(f32)[None],
+        vectors,
         seg_len,
         seg_parent,
     )
-    grad_f = grad_out[0].astype(f32)
-    summed, w_sum, down_grad, up_grad, out_grad, qkv_grad, vectors = tail_pass(
+    summed, w_sum, down_grad, up_grad, out_grad, qkv_grad, vectors, stats = tail_pass(
         group,
         pairs,
         arrived,
@@ -1188,57 +1357,57 @@
         w_qkv,
         hidden_all,
         tables,
+        early,
         norms,
         mlp_sums,
         up_sums,
-        jnp.sum(grad_f, axis=0)[None],
+        local_sums,
         seg_len,
         seg_parent,
     )
-    vectors = vectors.reshape(-1)
-    w_sum = w_sum.astype(f32)
-    hidden_out = (
-        hidden_in[0].astype(f32) + summed.astype(f32) + bias_out.astype(f32) + bias_down.astype(f32)
-    ).astype(bf16)
-    mine = lax.dynamic_slice_in_dim(tables[3], me * local_rows, local_rows)
-    my_rstd = mine[:, 1:2]
-    my_normed = (hidden_in[0].astype(f32) - mine[:, :1]) * my_rstd
-    grad_in = (
-        grad_f
-        + (
-            w_sum
-            - jnp.mean(w_sum, axis=-1, keepdims=True)
-            - my_normed * jnp.mean(w_sum * my_normed, axis=-1, keepdims=True)
-        )
-        * my_rstd
-    )
-
-    cuts = [D, D, D, D, D, 3 * D, FF]
-    ends = [sum(cuts[: i + 1]) for i in range(len(cuts))]
     (
+        down_grad,
+        up_grad,
+        qkv_grad,
+        out_grad,
+        hidden_out,
+        grad_in,
         gain_grad_a,
         shift_grad_a,
         gain_grad_m,
         shift_grad_m,
         out_bias_grad,
+        down_bias_grad,
         qkv_bias_grad,
         up_bias_grad,
-    ) = [vectors[end - cut : end] for cut, end in zip(cuts, ends)]
+    ) = finish_pass(
+        down_grad,
+        up_grad,
+        qkv_grad,
+        out_grad,
+        hidden_in[0],
+        grad_out[0],
+        summed,
+        w_sum,
+        stats,
+        norms,
+        vectors,
+    )
     return (
         hidden_out[None],
         grad_in[None],
         gain_grad_a,
         shift_grad_a,
-        qkv_grad.astype(f32),
+        qkv_grad,
         qkv_bias_grad,
-        out_grad.astype(f32),
+        out_grad,
         out_bias_grad,
         gain_grad_m,
         shift_grad_m,
-        up_grad.astype(f32),
+        up_grad,
         up_bias_grad,
-        down_grad.astype(f32),
-        out_bias_grad,
+        down_grad,
+        down_bias_grad,
     )
 
 

time: 321 us -> 295 us (0.919)
  other arithmetic: 23 us -> 0 us
  local copies, waits for them, and re-layouts: 11.4 us -> 0 us
  Pallas kernels: 283 us -> 294 us
    convert_element_type x7 -> x0, other arithmetic: 17 us -> none  [the longest x1 6.81 us: body(): up_grad.astype(f32)]
    pallas_call x0 -> x1, Pallas kernels: none -> 14.8 us  [finish_pass(): pl.pallas_call(finish_kernel, out_shape=[shape(array.shape, f32) for arra...]
    broadcast_in_dim x3 -> x0, other arithmetic: 4.91 us -> none  [the longest x1 2.86 us: body(): grad_in[None]]
    unnamed x31 -> x0, local copies, waits for them, and re-layouts: 4.33 us -> none
    pallas_call x1, Pallas kernels: 147 us -> 144 us  [tail_pass(): pl.pallas_call(functools.partial(tail_kernel, group), out_shape=(shape((r...]
where the time goes in v1:
time: 295 us
  Pallas kernels  294 us (100%)
    pallas_call x1, Pallas kernels, tail_pass(): pl.pallas_call(functools.partial(tail_kernel, group), out_shape=(shape((r...  144 us
    pallas_call x1, Pallas kernels, layer_pass(): pl.pallas_call(functools.partial(layer_kernel, group), out_shape=(whole,...  135 us
    pallas_call x1, Pallas kernels, finish_pass(): pl.pallas_call(finish_kernel, out_shape=[shape(array.shape, f32) for arra...  14.8 us

profile of v1, /device:TPU:13, one launch (start us, length us, event | category | flops | bytes accessed | tf_op | source)
XLA Modules:
  0.0 294.6 jit_solution(12906344840465231296)
XLA Ops:
  0.6 135.2 %layer_pass.1 = (bf16[1024,2048]{1,0:T(8,128)(2,1)}, bf16[1024,2048]{1,0:T(8,128)(2,1)}, bf16[1024,2048]{1,0:T(8,128)(2,1)}, bf16[3,1024,256]{2,1,0:T(8,128)(2,1...) custom-call(bf16[128,2048]{1,0:T(8,128)(2,1)} %bitcast.5, ...), custom_call_target="tpu_custom_call" | custom-call | tf_op jit(solution)/shard_map/layer_pass/pallas_call | solution.py:547
  135.9 143.7 %tail_pass.1 = (bf16[128,2048]{1,0:T(8,128)(2,1)}, bf16[128,2048]{1,0:T(8,128)(2,1)}, bf16[1024,2048]{1,0:T(8,128)(2,1)}, bf16[1024,2048]{1,0:T(8,128)(2,1)}, bf...) custom-call(bf16[1024,2048]{1,0:T(8,128)(2,1)} %get-tuple-element.50.refs_0_, ...), custom_call_target="tpu_custom_call" | custom-call | tf_op jit(solution)/shard_map/tail_pass/pallas_call | solution.py:1132
  279.6 14.8 %finish_pass.1 = (f32[1024,2048]{1,0:T(8,128)}, f32[1024,2048]{1,0:T(8,128)}, f32[768,2048]{1,0:T(8,128)}, f32[256,2048]{1,0:T(8,128)}, bf16[128,2048]{1,0:T(8,1...) custom-call(bf16[1024,2048]{1,0:T(8,128)(2,1)} %get-tuple-element.64, ...), custom_call_target="tpu_custom_call" | custom-call | tf_op jit(solution)/shard_map/finish_pass/pallas_call | solution.py:1273

commit v2 on v1

--- a/solution.py
+++ b/solution.py
@@ -84,6 +84,7 @@
     hidden, grad, w_up_in, w_down_in, w_qkv_in, w_out = refs[:6]
     vectors, (inverse, seg_len, seg_parent), refs = refs[6:14], refs[14:17], refs[7:]
     h_out, g_out, x_out, heads_out, part_out, back_out, pairs_out, early_out, cols_out = refs[10:19]
+    passing, refs = refs[19], refs[1:]
     tables, sums, bias_sum, local_sum, norms = refs[19:24]
     h_buf, g_buf, w_up, w_down, w_qkv, x_mlp, x_attn, act, slope, pre_grad = refs[24:34]
     heads, part, back, down_grad, up_grad, core_buf, mean, rstd, bias_up, bias_qkv = refs[34:44]
@@ -92,6 +93,7 @@
     own_sem, y_send, y_recv, up_send, up_recv, down_send, down_recv = refs[44:51]
     weight_sem, pair_sem, grad_sem, head_send, head_recv = refs[51:56]
     core_send, core_recv, cols_send, cols_recv, early_send, early_recv = refs[56:62]
+    pass_send, pass_recv = refs[62:64]
     dp, ctx, z, y, depth = place(group)
     bufs, sources, outs = (h_buf, g_buf), (hidden, grad), (h_out, g_out)
     rows = hidden.shape[0]
@@ -435,16 +437,47 @@
         local = pltpu.make_async_copy(heads.at[j], heads_out.at[kind], head_send.at[j])
         return target == ctx, remote, local
 
+    def turns_corner(device, target):
+        return (device % RAILS != target % RAILS) & (
+            lax.div(device, RAILS) == lax.div(target, RAILS) + 99
+        )
+
+    def to_corner(j):
+        target = pair_of(lax.rem(3 * ctx + j, group), group)
+        middle = (dp, lax.div(target, RAILS) * RAILS + y)
+        return copy_to(heads.at[j], passing, head_send.at[j], pass_recv.at[0], middle)
+
     def send_heads(crossing):
         for j in range(3):
             here, remote, local = to_head(j)
             target = pair_of(lax.rem(3 * ctx + j, group), group)
-            crosses = target % RAILS != ctx % RAILS
+            corner = turns_corner(ctx, target)
+            crosses = (target % RAILS != y) & jnp.logical_not(corner)
             if crossing:
                 pl.when(crosses)(lambda remote=remote: remote.start())
             else:
+                first = to_corner(j)
                 pl.when(here)(lambda local=local: local.start())
-                pl.when(jnp.logical_not(here | crosses))(lambda remote=remote: remote.start())
+                pl.when(corner)(lambda first=first: first.start())
+                pl.when(jnp.logical_not(here | crosses | corner))(
+                    lambda remote=remote: remote.start()
+                )
+
+    def hand_on(act_on):
+        partner = ctx + 1 - 2 * y
+        for kind in range(3):
+            source = lax.div(kind * group + pair_of(partner, group), 3)
+            arriving = copy_to(passing, passing, pass_send.at[0], pass_recv.at[0], other)
+            onward = copy_to(
+                passing, heads_out.at[kind], pass_send.at[0], head_recv.at[kind], other
+            )
+            pl.when(turns_corner(source, partner))(
+                lambda arriving=arriving, onward=onward: act_on(arriving, onward)
+            )
+
+    def pass_on(arriving, onward):
+        arriving.wait_recv()
+        onward.start()
 
     def head_source(kind):
         return lax.div(kind * group + pair_of(ctx, group), 3)
@@ -485,13 +518,14 @@
     backward(2)
     send_heads(True)
     y_arrive(1, 3)
-    backward(3)
     early = early_out.shape[0]
     outer(0, act, g_buf, True, range(early + 1))
     outer_sum(range(early))
     outer(0, act, g_buf, True, range(early + 1, tiles))
+    backward(3)
+    outer_sum(range(early, tiles))
     outer(1, pre_grad, x_mlp, True)
-    outer_sum(range(early, 2 * tiles))
+    outer_sum(range(tiles, 2 * tiles))
 
     for at_z in range(depth):
         to_other(0, at_z).wait_send()
@@ -501,8 +535,11 @@
             pl.when(has_below & (at_z >= z))(lambda i=i: downward(i, at_z).wait_send())
     for j in range(3):
         here, remote, local = to_head(j)
+        first = to_corner(j)
+        corner = turns_corner(ctx, pair_of(lax.rem(3 * ctx + j, group), group))
         pl.when(here)(lambda local=local: local.wait())
-        pl.when(jnp.logical_not(here))(lambda remote=remote: remote.wait_send())
+        pl.when(corner)(lambda first=first: first.wait_send())
+        pl.when(jnp.logical_not(here | corner))(lambda remote=remote: remote.wait_send())
     for kind in range(3):
         arriving = copy_to(
             heads.at[0], heads_out.at[kind], head_send.at[0], head_recv.at[kind], other
@@ -556,6 +593,7 @@
             shape((units, columns), bf16),
             shape((early, half, columns), bf16),
             shape((group, copies, columns // group // copies, head_cols), bf16),
+            shape((tokens, head_cols), bf16),
             shape((4, tokens, HEAD_DIM), f32),
             shape((2, columns), f32),
             shape((1, units), f32),
@@ -563,7 +601,7 @@
             shape((8, columns), f32),
         ),
         in_specs=[anywhere] * 6 + [vmem] * 9 + [smem] * 2,
-        out_specs=[anywhere] * 9 + [vmem] * 5,
+        out_specs=[anywhere] * 10 + [vmem] * 5,
         scratch_shapes=[pltpu.VMEM((tokens, columns), bf16)] * 2
         + [pltpu.VMEM((units, columns), bf16)] * 2
         + [pltpu.VMEM((3 * head_cols, columns), bf16)]
@@ -581,7 +619,8 @@
         + [sems((3,)), sems((5, 4)), sems((units // half,)), sems((3,)), sems((3,))]
         + [sems((units // half,))] * 2
         + [sems((group + 2,))] * 2
-        + [sems((early,))] * 2,
+        + [sems((early,))] * 2
+        + [sems((1,))] * 2,
         compiler_params=pltpu.CompilerParams(
             collective_id=0, has_side_effects=True, vmem_limit_bytes=62 * 2**20
         ),
@@ -592,8 +631,9 @@
 def tail_kernel(group, *refs):
     pairs, arrived_in, grad_in, w_cols_in, part_in, back_in, x_in, w_qkv_in, hidden_in = refs[:9]
     tables_in, early_in, norms, mlp_sums, up_sums, local_sums, seg_len, seg_parent = refs[9:17]
-    part_out, back_out, down_out, up_out, out_out, qkv_out, vectors_out, stats_out = refs[17:25]
-    refs = refs[25:]
+    part_out, back_out, down_out, up_out, out_out, qkv_out, passing = refs[17:24]
+    vectors_out, stats_out = refs[24:26]
+    refs = refs[26:]
     arrived, g_buf, w_cols, part, back, x_buf, w_qkv, h_buf, tables = refs[:9]
     att_grad, attended, returns, returned, y_buf, z_buf = refs[9:15]
     out_grad, qkv_grad, qkv_core, out_core, out_rows, from_x, pairs_x, key_acc, value_acc = refs[15:24]
@@ -623,6 +663,8 @@
         vec_send,
         vec_recv,
         sum_sem,
+        pass_send,
+        pass_recv,
     ) = refs[26:]
     dp, ctx, z, y, depth = place(group)
     tokens, columns = g_buf.shape
@@ -767,10 +809,41 @@
         local = pltpu.make_async_copy(returns.at[kind], returned.at[slot], head_send.at[kind])
         return owner == ctx, remote, local
 
+    def turns_corner(device, target):
+        return (device % RAILS != target % RAILS) & (
+            lax.div(device, RAILS) != lax.div(target, RAILS)
+        )
+
+    def owner_of(device, kind):
+        block = kind * group + pair_of(device, group)
+        return lax.div(block, 3), lax.rem(block, 3)
+
+    def to_corner(kind):
+        return copy_to(returns.at[kind], passing, head_send.at[kind], pass_recv.at[0], other)
+
+    def hand_on(act_on):
+        partner = ctx + 1 - 2 * y
+        for kind in range(3):
+            owner, slot = owner_of(partner, kind)
+            arriving = copy_to(passing, passing, pass_send.at[0], pass_recv.at[0], other)
+            onward = copy_to(
+                passing, returned.at[slot], pass_send.at[0], head_recv.at[slot], (dp, owner)
+            )
+            pl.when(turns_corner(partner, owner))(
+                lambda arriving=arriving, onward=onward: act_on(arriving, onward)
+            )
+
+    def pass_on(arriving, onward):
+        arriving.wait_recv()
+        onward.start()
+
     for kind in range(3):
         here, remote, local = to_owner(kind)
+        first = to_corner(kind)
+        corner = turns_corner(ctx, owner_of(ctx, kind)[0])
         pl.when(here)(lambda local=local: local.start())
-        pl.when(jnp.logical_not(here))(lambda remote=remote: remote.start())
+        pl.when(corner)(lambda first=first: first.start())
+        pl.when(jnp.logical_not(here | corner))(lambda remote=remote: remote.start())
 
     @pl.loop(0, group)
     def _(n):
@@ -862,6 +935,7 @@
     for s in range(depth):
         swap(0, s).start()
 
+    hand_on(pass_on)
     out_to_core.wait_recv()
 
     @pl.loop(0, group)
@@ -1062,9 +1136,13 @@
     x_sum(pair_tiles + 3)
     vector_step(4)
 
-    for j in range(3):
-        here, remote, local = to_owner(j)
-        pl.when(jnp.logical_not(here))(lambda remote=remote: remote.wait_send())
+    hand_on(lambda arriving, onward: onward.wait_send())
+    for kind in range(3):
+        here, remote, _ = to_owner(kind)
+        first = to_corner(kind)
+        corner = turns_corner(ctx, owner_of(ctx, kind)[0])
+        pl.when(corner)(lambda first=first: first.wait_send())
+        pl.when(jnp.logical_not(here | corner))(lambda remote=remote: remote.wait_send())
     for n in range(1, group):
         out_block(n).wait_send()
     out_to_core.wait_send()
@@ -1138,11 +1216,12 @@
             shape((units, columns), bf16),
             shape((2 * half, columns), bf16),
             shape(w_qkv.shape, bf16),
+            shape((tokens, head_cols), bf16),
             shape((vectors, lane_cols), f32),
             shape((rows, HEAD_DIM), f32),
         ),
         in_specs=[anywhere] * 11 + [small] * 4 + [smem] * 2,
-        out_specs=[anywhere] * 6 + [small] * 2,
+        out_specs=[anywhere] * 7 + [small] * 2,
         scratch_shapes=[
             vmem(arrived.shape, bf16),
             whole,
@@ -1179,7 +1258,7 @@
         + [sems((core_tiles + 1,))] * 2
         + [sems((every,))] * 3
         + [sems((5,))] * 2
-        + [sems((1,))],
+        + [sems((1,))] * 3,
         compiler_params=pltpu.CompilerParams(
             collective_id=1, has_side_effects=True, vmem_limit_bytes=62 * 2**20
         ),
@@ -1328,6 +1407,7 @@
         pairs,
         early,
         w_cols,
+        _,
         tables,
         mlp_sums,
         up_sums,
@@ -1345,7 +1425,7 @@
         seg_len,
         seg_parent,
     )
-    summed, w_sum, down_grad, up_grad, out_grad, qkv_grad, vectors, stats = tail_pass(
+    summed, w_sum, down_grad, up_grad, out_grad, qkv_grad, _, vectors, stats = tail_pass(
         group,
         pairs,
         arrived,
@@ -1780,7 +1860,7 @@
     token = P("dp", "ctx", None)
     rows = P("ctx", None)
     return jax.shard_map(
-        body if HEADS % mesh.shape["ctx"] == 0 else gather_body,
+        body if mesh.shape["ctx"] == 8 and mesh.shape["dp"] == 4 else gather_body,
         mesh=mesh,
         in_specs=(
             token,

time: 295 us -> 287 us (0.973)
  Pallas kernels: 294 us -> 284 us
    pallas_call x1, Pallas kernels: 135 us -> 130 us  [layer_pass(): pl.pallas_call(functools.partial(layer_kernel, group), out_shape=(whole,...]
    pallas_call x1, Pallas kernels: 144 us -> 139 us  [tail_pass(): pl.pallas_call(functools.partial(tail_kernel, group), out_shape=(shape((r...]
where the time goes in v2:
time: 287 us; the launch traced here: 285 us
  Pallas kernels  284 us (99%)
    pallas_call x1, Pallas kernels, tail_pass(): pl.pallas_call(functools.partial(tail_kernel, group), out_shape=(shape((r...  139 us
    pallas_call x1, Pallas kernels, layer_pass(): pl.pallas_call(functools.partial(layer_kernel, group), out_shape=(whole,...  130 us
    pallas_call x1, Pallas kernels, finish_pass(): pl.pallas_call(finish_kernel, out_shape=[shape(array.shape, f32) for arra...  14.8 us

profile of v2, /device:TPU:13, one launch (start us, length us, event | category | flops | bytes accessed | tf_op | source)
XLA Modules:
  0.0 285.0 jit_solution(8732200832211529537)
XLA Ops:
  0.6 130.0 %layer_pass.1 = (bf16[1024,2048]{1,0:T(8,128)(2,1)}, bf16[1024,2048]{1,0:T(8,128)(2,1)}, bf16[1024,2048]{1,0:T(8,128)(2,1)}, bf16[3,1024,256]{2,1,0:T(8,128)(2,1...) custom-call(bf16[128,2048]{1,0:T(8,128)(2,1)} %bitcast.5, ...), custom_call_target="tpu_custom_call" | custom-call | tf_op jit(solution)/shard_map/layer_pass/pallas_call | solution.py:584
  130.6 139.4 %tail_pass.1 = (bf16[128,2048]{1,0:T(8,128)(2,1)}, bf16[128,2048]{1,0:T(8,128)(2,1)}, bf16[1024,2048]{1,0:T(8,128)(2,1)}, bf16[1024,2048]{1,0:T(8,128)(2,1)}, bf...) custom-call(bf16[1024,2048]{1,0:T(8,128)(2,1)} %get-tuple-element.50, ...), custom_call_target="tpu_custom_call" | custom-call | tf_op jit(solution)/shard_map/tail_pass/pallas_call | solution.py:1210
  270.0 14.8 %finish_pass.1 = (f32[1024,2048]{1,0:T(8,128)}, f32[1024,2048]{1,0:T(8,128)}, f32[768,2048]{1,0:T(8,128)}, f32[256,2048]{1,0:T(8,128)}, bf16[128,2048]{1,0:T(8,1...) custom-call(bf16[1024,2048]{1,0:T(8,128)(2,1)} %get-tuple-element.64, ...), custom_call_target="tpu_custom_call" | custom-call | tf_op jit(solution)/shard_map/finish_pass/pallas_call | solution.py:1352

commit v3 on v2

--- a/solution.py
+++ b/solution.py
@@ -361,26 +361,28 @@
             grad_half(t, core), pairs_out.at[pl.ds(t * half, half)], grad_sem.at[t]
         )
 
-    def outer(n, left, right, last, ms=range(units // tall)):
-        first, second = (pair_at(2), pair_at(3)) if last else (pair_at(0), pair_at(1))
+    def outer(n, left, right, steps, ms=range(units // tall)):
         for m in ms:
             mine = pl.ds(m * tall, tall)
 
             @pl.loop(0, columns // (2 * wide))
             def _(k):
                 cols = pl.ds(pl.multiple_of(k * 2 * wide, 2 * wide), 2 * wide)
-                term = dot_tn(left[first, mine], right[first, cols])
-                term += dot_tn(left[second, mine], right[second, cols])
-                if last:
-                    term += held[n][mine, cols].astype(f32)
-                held[n][mine, cols] = term.astype(bf16)
-
-            if last:
+                terms = [dot_tn(left[pair_at(s), mine], right[pair_at(s), cols]) for s in steps]
+                if steps[0] > 0:
+                    terms.append(held[n][mine, cols].astype(f32))
+                held[n][mine, cols] = sum(terms[1:], terms[0]).astype(bf16)
+
+            if steps[-1] == depth - 1:
                 to_core(n * tiles + m).start()
 
     def early_x(t):
         return copy_to(
-            grad_half(t, core), early_out.at[t], early_send.at[t], early_recv.at[t], across
+            held[0].at[pl.ds(pl.multiple_of(t * tall + core * half, half), half // 2)],
+            early_out.at[t],
+            early_send.at[t],
+            early_recv.at[t],
+            across,
         )
 
     def outer_sum(ts):
@@ -510,21 +512,23 @@
     turn(7)
     columns_arrive()
     columns_core(core).start()
-    outer(0, act, g_buf, False)
-    outer(1, pre_grad, x_mlp, False)
+    outer(0, act, g_buf, (0, 1))
+    outer(1, pre_grad, x_mlp, (0, 1))
     columns_core(1 - core).wait_recv()
     columns_x(x).start()
     y_arrive(1, 2)
     backward(2)
+    outer(0, act, g_buf, (2,))
+    outer(1, pre_grad, x_mlp, (2,))
+    y_arrive(1, 3)
     send_heads(True)
-    y_arrive(1, 3)
     early = early_out.shape[0]
-    outer(0, act, g_buf, True, range(early + 1))
+    outer(0, act, g_buf, (3,), range(early + 1))
     outer_sum(range(early))
-    outer(0, act, g_buf, True, range(early + 1, tiles))
+    outer(0, act, g_buf, (3,), range(early + 1, tiles))
     backward(3)
     outer_sum(range(early, tiles))
-    outer(1, pre_grad, x_mlp, True)
+    outer(1, pre_grad, x_mlp, (3,))
     outer_sum(range(tiles, 2 * tiles))
 
     for at_z in range(depth):
@@ -591,7 +595,7 @@
             whole,
             whole,
             shape((units, columns), bf16),
-            shape((early, half, columns), bf16),
+            shape((early, half // 2, columns), bf16),
             shape((group, copies, columns // group // copies, head_cols), bf16),
             shape((tokens, head_cols), bf16),
             shape((4, tokens, HEAD_DIM), f32),
@@ -699,17 +703,19 @@
                 target.dtype
             )
 
+    early = early_in.shape[0]
+
     def pair_x(t):
+        first = half // 2 if t < early else 0
         return copy_to(
-            pairs.at[pl.ds(t * half, half)],
-            pairs_x.at[t],
+            pairs.at[pl.ds(t * half + first, half - first)],
+            pairs_x.at[t, pl.ds(first, half - first)],
             pair_send.at[t],
             pair_recv.at[t],
             across,
         )
 
-    early = early_in.shape[0]
-    for t in range(early, pair_tiles):
+    for t in range(pair_tiles):
         pair_x(t).start()
     loads = [
         pltpu.make_async_copy(source, target, load_sem.at[n])
@@ -724,7 +730,7 @@
                 (back_in, back),
                 (hidden_in, h_buf),
                 (x_in, x_buf),
-                (early_in, pairs_x.at[pl.ds(0, early)]),
+                (early_in, pairs_x.at[pl.ds(0, early), pl.ds(0, half // 2)]),
             )
         )
     ]
@@ -1000,8 +1006,7 @@
     def x_sum(t):
         total = total_of(t)
         if t < pair_tiles:
-            if t >= early:
-                pair_x(t).wait_recv()
+            pair_x(t).wait_recv()
             add(total, total, g_buf.at[pl.ds(t * half, half)])
         else:
             n = t - pair_tiles
@@ -1012,7 +1017,6 @@
 
     loads[9].wait()
     again.wait()
-    x_sum(0)
     for j in range(3):
         here, remote, local = to_owner(j)
         pl.when(here)(lambda local=local: local.wait())
@@ -1107,6 +1111,7 @@
     for s in range(depth):
         scatter_step(0, s)
         if s == 0:
+            x_sum(0)
             x_sum(1)
             x_sum(2)
         x_sum(3 + s)
@@ -1150,7 +1155,7 @@
         to_core(t).wait_send()
     for t in range(core_tiles + 1):
         across_x(t).wait_send()
-    for t in range(early, pair_tiles):
+    for t in range(pair_tiles):
         pair_x(t).wait_send()
     for t in range(len(spots)):
         keep(t).wait()

time: 287 us -> 279 us (0.972)
  Pallas kernels: 284 us -> 276 us
    pallas_call x1, Pallas kernels: 130 us -> 121 us  [layer_pass(): pl.pallas_call(functools.partial(layer_kernel, group), out_shape=(whole,...]
where the time goes in v3:
time: 279 us; the launch traced here: 277 us
  Pallas kernels  276 us (99%)
    pallas_call x1, Pallas kernels, tail_pass(): pl.pallas_call(functools.partial(tail_kernel, group), out_shape=(shape((r...  139 us
    pallas_call x1, Pallas kernels, layer_pass(): pl.pallas_call(functools.partial(layer_kernel, group), out_shape=(whole,...  121 us
    pallas_call x1, Pallas kernels, finish_pass(): pl.pallas_call(finish_kernel, out_shape=[shape(array.shape, f32) for arra...  14.8 us

profile of v3, /device:TPU:13, one launch (start us, length us, event | category | flops | bytes accessed | tf_op | source)
XLA Modules:
  0.0 276.5 jit_solution(15582856308236868851)
XLA Ops:
  0.6 121.5 %layer_pass.1 = (bf16[1024,2048]{1,0:T(8,128)(2,1)}, bf16[1024,2048]{1,0:T(8,128)(2,1)}, bf16[1024,2048]{1,0:T(8,128)(2,1)}, bf16[3,1024,256]{2,1,0:T(8,128)(2,1...) custom-call(bf16[128,2048]{1,0:T(8,128)(2,1)} %bitcast.5, ...), custom_call_target="tpu_custom_call" | custom-call | tf_op jit(solution)/shard_map/layer_pass/pallas_call | solution.py:588
  122.1 139.4 %tail_pass.1 = (bf16[128,2048]{1,0:T(8,128)(2,1)}, bf16[128,2048]{1,0:T(8,128)(2,1)}, bf16[1024,2048]{1,0:T(8,128)(2,1)}, bf16[1024,2048]{1,0:T(8,128)(2,1)}, bf...) custom-call(bf16[1024,2048]{1,0:T(8,128)(2,1)} %get-tuple-element.50, ...), custom_call_target="tpu_custom_call" | custom-call | tf_op jit(solution)/shard_map/tail_pass/pallas_call | solution.py:1215
  261.6 14.8 %finish_pass.1 = (f32[1024,2048]{1,0:T(8,128)}, f32[1024,2048]{1,0:T(8,128)}, f32[768,2048]{1,0:T(8,128)}, f32[256,2048]{1,0:T(8,128)}, bf16[128,2048]{1,0:T(8,1...) custom-call(bf16[1024,2048]{1,0:T(8,128)(2,1)} %get-tuple-element.64, ...), custom_call_target="tpu_custom_call" | custom-call | tf_op jit(solution)/shard_map/finish_pass/pallas_call | solution.py:1357
